TPU v7x, 32 devices: a whole 2x2x4 slice. The times are simulated.
32 devices in a mesh: dp: 4 (over z), ctx: 2 (over x), tp: 4 (over y, core).
Axes of the slice: x: 2, y: 2, z: 4, core: 2. Of those that a mesh axis runs over, the one named last changes fastest.
Arguments:
- tokens: bfloat16 [8192, 1024], P(('dp', 'ctx')), may hold values from -6 to 6
- cotangent: bfloat16 [8192, 1024], P(('dp', 'ctx')), may hold values from -6 to 6
- lengths: int32 [4, 4], P('dp'), may hold values from 1 to 2048, as said below
- norm1_gain: float32 [1024], replicated, may hold values from 0.5 to 1.5
- norm2_gain: float32 [1024], replicated, may hold values from 0.5 to 1.5
- query_proj: bfloat16 [1024, 512], P(('dp', 'ctx'), 'tp'), may hold values from -0.1875 to 0.1875
- keyval_proj: bfloat16 [1024, 2, 128], P(('dp', 'ctx')), may hold values from -0.1875 to 0.1875
- attn_proj: bfloat16 [512, 1024], P('tp', ('dp', 'ctx')), may hold values from -1 to 1
- inner_proj: bfloat16 [1024, 2, 1536], P(('dp', 'ctx'), None, 'tp'), may hold values from -0.1875 to 0.1875
- state_proj: bfloat16 [1024, 2, 128], P(('dp', 'ctx')), may hold values from -0.1875 to 0.1875
- step_proj: bfloat16 [1024, 24], P(('dp', 'ctx'), 'tp'), may hold values from -0.1875 to 0.1875
- conv_inner: float32 [5, 1536], replicated, may hold values from -3 to 3
- conv_state: float32 [5, 2, 128], replicated, may hold values from -3 to 3
- step_bias: float32 [24], replicated, may hold values from -9 to -2
- decay_log: float32 [24], replicated, may hold values from -1 to 1
- skip_gain: float32 [24], replicated, may hold values from 0.5 to 1.5
- mamba_gain: float32 [1536], replicated, may hold values from 0.5 to 1.5
- mamba_proj: bfloat16 [1536, 1024], P('tp', ('dp', 'ctx')), may hold values from -0.15625 to 0.15625
- gateup_proj: bfloat16 [1024, 2, 2048], P(('dp', 'ctx'), None, 'tp'), may hold values from -0.1875 to 0.1875
- down_proj: bfloat16 [2048, 1024], P('tp', ('dp', 'ctx')), may hold values from -0.125 to 0.125
Outputs:
- layer_out: bfloat16 [8192, 1024], P(('dp', 'ctx'))
- tokens_grad: bfloat16 [8192, 1024], P(('dp', 'ctx'))
- norm1_grad: float32 [1024], replicated
- norm2_grad: float32 [1024], replicated
- query_grad: float32 [1024, 512], P(('dp', 'ctx'), 'tp')
- keyval_grad: float32 [1024, 2, 128], P(('dp', 'ctx'))
- attn_grad: float32 [512, 1024], P('tp', ('dp', 'ctx'))
- inner_grad: float32 [1024, 2, 1536], P(('dp', 'ctx'), None, 'tp')
- state_grad: float32 [1024, 2, 128], P(('dp', 'ctx'))
- step_grad: float32 [1024, 24], P(('dp', 'ctx'), 'tp')
- convin_grad: float32 [5, 1536], replicated
- convst_grad: float32 [5, 2, 128], replicated
- stepbias_grad: float32 [24], replicated
- decay_grad: float32 [24], replicated
- skip_grad: float32 [24], replicated
- mgain_grad: float32 [1536], replicated
- mamba_grad: float32 [1536, 1024], P('tp', ('dp', 'ctx'))
- gateup_grad: float32 [1024, 2, 2048], P(('dp', 'ctx'), None, 'tp')
- down_grad: float32 [2048, 1024], P('tp', ('dp', 'ctx'))
Inputs may be any that keep to these rules, and one draw needn't show every extreme that they name: Row r lists, in order, the lengths of the 4 documents packed into the 2048 tokens of dp index r; each row sums to 2048.
All inputs are finite; a program needn't handle non-finite values.
Results may differ from a plain program's by a relative error of at most 0.03.
Values may be sent and summed in bfloat16 or wider, within the bound.
No kernel may reach another device: no remote copies, remote signals or barrier semaphores. Data moves between devices by JAX's collectives and lax.ppermute only.
A program may use at most 192 MiB of HBM per device.

v0:
```python
import functools

import jax
import jax.numpy as jnp
from jax import lax
from jax.experimental import pallas as pl
from jax.experimental.layout import Layout, with_layout_constraint
from jax.experimental.pallas import tpu as pltpu
from jax.sharding import PartitionSpec as P

H = 8
KVH = 2
HD = 64
PD = 64
NST = 128
CONV = 4
CHUNK = 256
QUERY_BLOCK = 256
KEY_BLOCK = 512
EDGE = 8
LANES = 128
VMEM_BYTES = 48 * 1024 * 1024

EPS = 1e-05
ROPE_BASE = 10000.0
MASKED = -1e30
HIGH = lax.Precision.HIGHEST
F32 = jnp.float32
BF16 = jnp.bfloat16
WEIGHT_AXES = ("dp", "ctx")


def product(left, right):
    return jnp.dot(left, right, preferred_element_type=F32)


def product_tn(left, right):
    return lax.dot_general(left, right, (((0,), (0,)), ((), ())), preferred_element_type=F32)


def product_nt(left, right):
    return lax.dot_general(left, right, (((1,), (1,)), ((), ())), preferred_element_type=F32)


def low_nn(left, right):
    return product(left.astype(BF16), right.astype(BF16))


def low_tn(left, right):
    return product_tn(left.astype(BF16), right.astype(BF16))


def low_nt(left, right):
    return product_nt(left.astype(BF16), right.astype(BF16))


def split_nn(left, ones):
    first = left.astype(BF16)
    second = (left - first.astype(F32)).astype(BF16)
    return product(first, ones) + product(second, ones)


def split_nt(ones, right):
    first = right.astype(BF16)
    second = (right - first.astype(F32)).astype(BF16)
    return product_nt(ones, first) + product_nt(ones, second)


def iota(shape, dim):
    return lax.broadcasted_iota(jnp.int32, shape, dim)


def start_of(rows, meta, docs):
    start = jnp.full(rows.shape, meta[0], jnp.int32)
    for doc in range(1, docs):
        start = jnp.where(rows >= meta[doc], meta[doc], start)
    return start


def start_of_one(row, meta, docs):
    start = meta[0]
    for doc in range(1, docs):
        start = jnp.where(row >= meta[doc], meta[doc], start)
    return start


def sigmoid(values):
    return 1.0 / (1.0 + jnp.exp(-values))


def swap_halves(values):
    lane = iota(values.shape, 1)
    up = pltpu.roll(values, LANES - HD // 2, 1)
    down = pltpu.roll(values, HD // 2, 1)
    return jnp.where(lane % HD < HD // 2, up, down)


def prep_kernel(
    docs,
    inner_width,
    meta,
    proj,
    edge,
    taps,
    heads,
    cosine,
    sine,
    spread,
    spread_t,
    q_out,
    kv_out,
    mixed_out,
    act_out,
    slope_out,
    step_out,
    sig_out,
    cum_out,
    state_out,
    end_out,
    ext,
    state,
    total_log,
):
    c = pl.program_id(0)
    rows = proj.shape[0]
    mix = ext.shape[1]
    row = c * rows + iota((rows, 1), 0)
    rel = row - start_of(row, meta, docs)
    mixed = proj[:, :mix].astype(BF16)
    mixed_out[...] = mixed

    @pl.when(c == 0)
    def _():
        ext[0:EDGE] = edge[...]
        state[...] = jnp.zeros_like(state)
        total_log[...] = jnp.zeros_like(total_log)

    @pl.when(c > 0)
    def _():
        ext[0:EDGE] = ext[rows : rows + EDGE]

    ext[EDGE : EDGE + rows] = mixed.astype(F32)
    pre = jnp.broadcast_to(taps[CONV : CONV + 1, :], (rows, mix))
    for lag in range(CONV):
        keep = (rel >= lag).astype(F32)
        pre = pre + taps[CONV - 1 - lag : CONV - lag, :] * (
            ext[EDGE - lag : EDGE - lag + rows] * keep
        )
    sig = sigmoid(pre)
    act = pre * sig
    act_out[...] = act
    slope_out[...] = sig * (1.0 + pre * (1.0 - sig))

    base = mix
    cos, sin = (cosine[...], sine[...])
    queries = proj[:, base : base + LANES]
    turned = queries * cos + swap_halves(queries) * sin
    q_out[...] = (turned * HD ** (-0.5)).astype(BF16)
    keyval = proj[:, base + LANES : base + 2 * LANES]
    is_key = iota(keyval.shape, 1) < HD
    kv_out[...] = jnp.where(is_key, keyval * cos + swap_halves(keyval) * sin, keyval).astype(BF16)

    raw = proj[:, base + 2 * LANES : base + 3 * LANES] + heads[0:1, :]
    step = jnp.maximum(raw, 0.0) + jnp.log1p(jnp.exp(-jnp.abs(raw)))
    decay = -step * heads[1:2, :]
    lower = (iota((rows, rows), 0) >= iota((rows, rows), 1)).astype(F32)
    cum = jnp.dot(lower, decay, precision=HIGH, preferred_element_type=F32)
    step_out[...] = step
    sig_out[...] = sigmoid(raw)
    cum_out[...] = cum

    last = c * rows + rows - 1
    last_start = start_of_one(last, meta, docs)
    total = cum[rows - 1 : rows, :]
    tail = jnp.where(row >= last_start, jnp.exp(total - cum), 0.0) * step
    goes_on = jnp.where(last_start < c * rows, 1.0, 0.0)
    kept = split_nt(spread_t[...], jnp.broadcast_to(jnp.exp(total) * goes_on, (NST, LANES)))
    state_out[...] = state[...]
    added = low_tn(act[:, :inner_width] * split_nn(tail, spread[...]), act[:, inner_width : inner_width + NST])
    state[...] = kept * state[...] + added
    total_log[...] = total_log[...] + jnp.broadcast_to(total, total_log.shape)

    @pl.when(c == pl.num_programs(0) - 1)
    def _():
        through = jnp.exp(total_log[0:1, :]) * jnp.where(last_start < 0, 1.0, 0.0)
        first = through.astype(BF16)
        second = (through - first.astype(F32)).astype(BF16)
        sub = iota((16, LANES), 0)
        end_out[0:inner_width] = state[...].astype(BF16)
        end_out[inner_width : inner_width + 16] = jnp.where(
            sub == 0, first.astype(F32), jnp.where(sub == 1, second.astype(F32), 0.0)
        ).astype(BF16)


def intra_kernel(docs, inner_width, meta, act, step, cum, spread, y_out):
    c = pl.program_id(0)
    rows = act.shape[0]
    row = iota((rows, 1), 0)
    first = start_of(c * rows + row, meta, docs) - c * rows
    col = iota((rows, rows), 1)
    linked = (col >= first) & (col <= iota((rows, rows), 0))
    couple = low_nt(act[:, inner_width + NST :], act[:, inner_width : inner_width + NST])
    weighted = (act[:, :inner_width] * split_nn(step[...], spread[...])).astype(BF16)
    cum_now = cum[...]
    cum_t = cum_now.T
    lane = iota((rows, LANES), 1)
    for pair in range(inner_width // LANES):
        values = weighted[:, pair * LANES : (pair + 1) * LANES]
        results = []
        for head in (2 * pair, 2 * pair + 1):
            arg = cum_now[:, head : head + 1] - cum_t[head : head + 1, :]
            mixing = couple * jnp.exp(jnp.where(linked, arg, MASKED))
            results.append(product(mixing.astype(BF16), values))
        y_out[:, pair * LANES : (pair + 1) * LANES] = jnp.where(lane < PD, results[0], results[1])


def two_heads(values, upper):
    values = values.astype(F32)
    lane = iota(values.shape, 1)
    rolled = pltpu.roll(values, HD, 1)
    keep = lane >= HD if upper else lane < HD
    pair = (rolled, values) if upper else (values, rolled)
    return jnp.concatenate([jnp.where(keep, part, 0.0) for part in pair], axis=0)


def attend_kernel(docs, meta, q, kv, out, lse_out):
    block = pl.program_id(0)
    rows = q.shape[0]
    first_row = meta[docs]
    row = block * rows + iota((rows, 1), 0)
    start = start_of(row, meta, docs)
    queries = two_heads(q[...], False).astype(BF16)
    low_block = (start_of_one(block * rows, meta, docs) + first_row) // KEY_BLOCK
    high_block = (first_row + (block + 1) * rows + KEY_BLOCK - 1) // KEY_BLOCK

    def one(index, sums):
        top, total, summed = sums
        at = pl.multiple_of(index * KEY_BLOCK, KEY_BLOCK)
        keyval = kv[pl.ds(at, KEY_BLOCK), :]
        scores = product_nt(queries, keyval)
        key = index * KEY_BLOCK - first_row + iota((rows, KEY_BLOCK), 1)
        allowed = (key >= start) & (key <= row)
        allowed = jnp.concatenate([allowed, allowed], axis=0)
        scores = jnp.where(allowed, scores, MASKED)
        new_top = jnp.maximum(top, jnp.max(scores, axis=1, keepdims=True))
        scale = jnp.exp(top - new_top)
        probs = jnp.exp(scores - new_top)
        total = total * scale + jnp.sum(probs, axis=1, keepdims=True)
        return (new_top, total, summed * scale + product(probs.astype(BF16), keyval))

    top, total, summed = lax.fori_loop(
        low_block,
        high_block,
        one,
        (
            jnp.full((2 * rows, 1), MASKED, F32),
            jnp.zeros((2 * rows, 1), F32),
            jnp.zeros((2 * rows, LANES), F32),
        ),
    )
    result = summed / total
    lse = top + jnp.log(total)
    lane = iota((rows, LANES), 1)
    out[...] = jnp.where(lane < HD, pltpu.roll(result[:rows], HD, 1), result[rows:]).astype(BF16)
    lse_out[...] = jnp.where(lane < HD, lse[:rows], lse[rows:])


def attend_back_kernel(docs, meta, q, kv, grad, att, lse, cosine, sine, gq_out, gkv_out):
    block = pl.program_id(0)
    rows = q.shape[0]
    first_row = meta[docs]

    @pl.when(block == 0)
    def _():
        gkv_out[...] = jnp.zeros_like(gkv_out)

    row = block * rows + iota((rows, 1), 0)
    start = start_of(row, meta, docs)
    queries = two_heads(q[...], False).astype(BF16)
    grads = two_heads(grad[...].astype(BF16), True)
    lse_now = lse[...]
    lse_col = jnp.concatenate([lse_now[:, 0:1], lse_now[:, HD : HD + 1]], axis=0)
    delta = jnp.sum(grads * two_heads(att[...], True), axis=1, keepdims=True)
    grads = grads.astype(BF16)
    low_block = (start_of_one(block * rows, meta, docs) + first_row) // KEY_BLOCK
    high_block = (first_row + (block + 1) * rows + KEY_BLOCK - 1) // KEY_BLOCK

    def one(index, summed):
        at = pl.multiple_of(index * KEY_BLOCK, KEY_BLOCK)
        keyval = kv[pl.ds(at, KEY_BLOCK), :]
        scores = product_nt(queries, keyval)
        key = index * KEY_BLOCK - first_row + iota((rows, KEY_BLOCK), 1)
        allowed = (key >= start) & (key <= row)
        allowed = jnp.concatenate([allowed, allowed], axis=0)
        probs = jnp.exp(jnp.where(allowed, scores - lse_col, MASKED))
        grad_scores = (probs * (product_nt(grads, keyval) - delta)).astype(BF16)
        gkv_out[pl.ds(at, KEY_BLOCK), :] += product_tn(grad_scores, queries) + product_tn(
            probs.astype(BF16), grads
        )
        return summed + product(grad_scores, keyval)

    summed = lax.fori_loop(low_block, high_block, one, jnp.zeros((2 * rows, LANES), F32))
    lane = iota((rows, LANES), 1)
    grad_q = jnp.where(lane < HD, summed[:rows], pltpu.roll(summed[rows:], HD, 1)) * HD ** (-0.5)
    gq_out[...] = (grad_q * cosine[...] - swap_halves(grad_q) * sine[...]).astype(BF16)


def finish_kernel(
    docs,
    inner_width,
    meta,
    y_in,
    act,
    cum,
    gate,
    att,
    state_local,
    state_in,
    params,
    spread,
    spread_t,
    block_ones,
    low_out,
    y_out,
    state_out,
    carry,
):
    c = pl.program_id(0)
    rows = act.shape[0]

    @pl.when(c == 0)
    def _():
        carry[...] = state_in[...]

    row = c * rows + iota((rows, 1), 0)
    start = start_of(row, meta, docs)
    last_start = start_of_one(c * rows + rows - 1, meta, docs)
    cum_now = cum[...]
    inflow = jnp.where(start < c * rows, jnp.exp(cum_now), 0.0)
    state = state_local[...] + carry[...]
    state_out[...] = state
    inner = act[:, :inner_width]
    y = y_in[...] + low_nt(act[:, inner_width + NST :], state) * split_nn(inflow, spread[...])
    y_out[...] = y
    total = jnp.exp(cum_now[rows - 1 : rows, :]) * jnp.where(last_start < c * rows, 1.0, 0.0)
    carry[...] = carry[...] * split_nt(spread_t[...], jnp.broadcast_to(total, (NST, LANES)))
    gate_now = gate[...]
    gated = (y + params[0:1, :] * inner) * (gate_now * sigmoid(gate_now))
    mean = split_nn(gated * gated, block_ones[...]) * (1.0 / PD)
    low = gated * lax.rsqrt(mean + EPS) * params[1:2, :]
    low_out[:, :LANES] = att[...]
    low_out[:, LANES:] = low.astype(BF16)


def finish_back_kernel(
    docs,
    inner_width,
    meta,
    grad,
    y_in,
    act,
    cum,
    gate,
    params,
    spread,
    block_ones,
    gy_out,
    gate_out,
    params_out,
    state_out,
    so_far,
):
    c = pl.program_id(0)
    rows = act.shape[0]

    @pl.when(c == 0)
    def _():
        params_out[...] = jnp.zeros_like(params_out)
        state_out[...] = jnp.zeros_like(state_out)
        so_far[...] = jnp.zeros_like(so_far)

    row = c * rows + iota((rows, 1), 0)
    start = start_of(row, meta, docs)
    cum_now = cum[...]
    inner = act[:, :inner_width]
    skip, gain = (params[0:1, :], params[1:2, :])
    gate_now = gate[...]
    sig = sigmoid(gate_now)
    silu = gate_now * sig
    with_skip = y_in[...] + skip * inner
    gated = with_skip * silu
    ones = block_ones[...]
    scale = lax.rsqrt(split_nn(gated * gated, ones) * (1.0 / PD) + EPS)
    grad_now = grad[...]
    unit = gated * scale
    grad_unit = grad_now * gain
    mean = split_nn(grad_unit * unit, ones) * (1.0 / PD)
    grad_gated = scale * (grad_unit - unit * mean)
    grad_y = grad_gated * silu
    gy_out[...] = grad_y
    gate_out[...] = (grad_gated * with_skip * (sig * (1.0 + gate_now * (1.0 - sig)))).astype(BF16)
    params_out[0:1, :] += jnp.sum(grad_y * inner, axis=0, keepdims=True)
    params_out[1:2, :] += jnp.sum(grad_now * unit, axis=0, keepdims=True)
    inflow = jnp.where(start < 0, jnp.exp(cum_now + so_far[0:1, :]), 0.0)
    state_out[...] += low_tn(grad_y * split_nn(inflow, spread[...]), act[:, inner_width + NST :])
    so_far[...] = so_far[...] + jnp.broadcast_to(cum_now[rows - 1 : rows, :], so_far.shape)


def scan_back_kernel(
    docs,
    inner_width,
    meta,
    act,
    slope,
    step_in,
    sig_in,
    cum,
    grad_y_in,
    state_in,
    grad_end,
    mixed,
    edge,
    taps,
    heads,
    params,
    spread,
    spread_t,
    gmix_out,
    gstep_out,
    tail_out,
    edge_out,
    taps_out,
    heads_out,
    ext,
    grad_state,
):
    c = pl.num_programs(0) - 1 - pl.program_id(0)
    rows = act.shape[0]

    @pl.when(pl.program_id(0) == 0)
    def _():
        grad_state[...] = grad_end[...]
        ext[0:EDGE] = jnp.zeros((EDGE, ext.shape[1]), F32)
        ext[EDGE + rows :] = jnp.zeros((EDGE, ext.shape[1]), F32)
        taps_out[...] = jnp.zeros_like(taps_out)
        heads_out[...] = jnp.zeros_like(heads_out)

    @pl.when(pl.program_id(0) > 0)
    def _():
        ext[EDGE + rows :] = ext[EDGE : 2 * EDGE]

    at = c * rows
    row = at + iota((rows, 1), 0)
    start = start_of(row, meta, docs)
    last_start = start_of_one(at + rows - 1, meta, docs)
    inner = act[:, :inner_width]
    write = act[:, inner_width : inner_width + NST].astype(BF16)
    read = act[:, inner_width + NST :].astype(BF16)
    step = step_in[...]
    cum_now = cum[...]
    grad_y = grad_y_in[...]
    spread_now = spread[...]
    spread_back = spread_t[...]
    state = state_in[...]
    grads = grad_state[...]
    total = cum_now[rows - 1 : rows, :]
    step_wide = split_nn(step, spread_now)
    weighted = inner * step_wide
    tail = split_nn(jnp.where(row >= last_start, jnp.exp(total - cum_now), 0.0), spread_now)
    inflow = split_nn(jnp.where(start < at, jnp.exp(cum_now), 0.0), spread_now)
    kept_row = jnp.exp(total) * jnp.where(last_start < at, 1.0, 0.0)

    grads_low = grads.astype(BF16)
    state_low = state.astype(BF16)
    from_state = tail * product_nt(write, grads_low)
    leaving = split_nn(weighted * from_state, spread_back)
    grad_write = low_nn(tail * weighted, grads_low)
    arriving_y = inflow * grad_y
    arriving_low = arriving_y.astype(BF16)
    grad_read = product(arriving_low, state_low)
    arriving = split_nn(arriving_y * product_nt(read, state_low), spread_back)
    grad_state[...] = split_nt(
        spread_back, jnp.broadcast_to(kept_row, (NST, LANES))
    ) * grads + product_tn(arriving_low, read)
    both = split_nt(jnp.ones((8, NST), BF16), grads * state)
    kept_grad = kept_row * split_nn(both, spread_back)[0:1, :]
    grad_total = kept_grad + jnp.sum(leaving, axis=0, keepdims=True)

    couple_t = product_nt(write, read)
    at_key = iota((rows, rows), 0)
    at_query = iota((rows, rows), 1)
    end_row = at + iota((1, rows), 1)
    start_row = start_of(end_row, meta, docs) - at
    linked = (at_key >= start_row) & (at_key <= at_query)
    cum_t = cum_now.T
    lane = iota((rows, LANES), 1)
    sub = iota((LANES, rows), 0)
    weighted_low = weighted.astype(BF16)
    grad_y_low = grad_y.astype(BF16)
    grad_couple = jnp.zeros((rows, rows), F32)
    grad_cum = arriving - leaving
    grad_cum_t = jnp.zeros((LANES, rows), F32)
    pieces = []
    for pair in range(inner_width // LANES):
        span = slice(pair * LANES, (pair + 1) * LANES)
        values = weighted_low[:, span]
        grads_here = grad_y_low[:, span]
        results = []
        for side in range(2):
            head = 2 * pair + side
            arg = cum_t[head : head + 1, :] - cum_now[:, head : head + 1]
            decay = jnp.exp(jnp.where(linked, arg, MASKED))
            mine = jnp.where((lane >= PD) == (side == 1), values, jnp.zeros_like(values))
            grad_mixing = product_nt(mine, grads_here) * decay
            grad_couple = grad_couple + grad_mixing
            by_log = grad_mixing * couple_t
            grad_cum = grad_cum - jnp.where(
                lane == head, jnp.sum(by_log, axis=1, keepdims=True), 0.0
            )
            grad_cum_t = grad_cum_t + jnp.where(
                sub == head, jnp.sum(by_log, axis=0, keepdims=True), 0.0
            )
            results.append(product((couple_t * decay).astype(BF16), grads_here))
        pieces.append(jnp.where(lane < PD, results[0], results[1]))
    grad_weighted = jnp.concatenate(pieces, axis=1) + from_state
    grad_couple_low = grad_couple.astype(BF16)
    grad_write = grad_write + product(grad_couple_low, read)
    grad_read = grad_read + product_tn(grad_couple_low, write)

    grad_cum = grad_cum + grad_cum_t.T
    upper = (at_query >= at_key).astype(F32)
    grad_decay = (
        jnp.dot(upper, grad_cum, precision=HIGH, preferred_element_type=F32) + grad_total
    )
    rate = heads[1:2, :]
    grad_inner = grad_weighted * step_wide + grad_y * params[0:1, :]
    grad_step = split_nn(grad_weighted * inner, spread_back) - grad_decay * rate
    grad_raw = grad_step * sig_in[...]
    gstep_out[...] = grad_raw.astype(BF16)
    heads_out[0:1, :] += jnp.sum(grad_raw, axis=0, keepdims=True)
    heads_out[1:2, :] += jnp.sum(grad_decay * (-step * rate), axis=0, keepdims=True)

    grad_pre = jnp.concatenate([grad_inner, grad_write, grad_read], axis=1) * slope[...]
    ext[EDGE : EDGE + rows] = grad_pre
    taps_out[CONV : CONV + 1, :] += jnp.sum(grad_pre, axis=0, keepdims=True)
    mixed_now = mixed[...].astype(F32)
    grad_mixed = jnp.zeros_like(grad_pre)
    for lag in range(CONV):
        target = row + lag
        keep = (target - start_of(target, meta, docs) >= lag).astype(F32)
        moved = ext[EDGE + lag : EDGE + lag + rows] * keep
        grad_mixed = grad_mixed + taps[CONV - 1 - lag : CONV - lag, :] * moved
        taps_out[CONV - 1 - lag : CONV - lag, :] += jnp.sum(
            moved * mixed_now, axis=0, keepdims=True
        )
    gmix_out[...] = grad_mixed.astype(BF16)

    @pl.when(pl.program_id(0) == 0)
    def _():
        tail_out[...] = grad_mixed[rows - EDGE :]

    @pl.when(c == 0)
    def _():
        before = iota((EDGE, 1), 0) - EDGE
        edge_now = edge[...]
        grad_edge = jnp.zeros_like(edge_now)
        for lag in range(1, CONV):
            target = before + lag
            keep = (target - start_of(target, meta, docs) >= lag).astype(F32)
            moved = ext[lag : lag + EDGE] * keep
            grad_edge = grad_edge + taps[CONV - 1 - lag : CONV - lag, :] * moved
            taps_out[CONV - 1 - lag : CONV - lag, :] += jnp.sum(
                moved * edge_now, axis=0, keepdims=True
            )
        edge_out[...] = grad_edge


def feed_kernel(ff, normed, cotangent, weights, act_out, grad_out, back_out, forward_out):
    gateup_w = weights[:, : 2 * ff]
    down_w = weights[:, 2 * ff :]
    grad_hidden = product(cotangent[...], down_w)
    gateup = product(normed[...], gateup_w)
    gate, up = (gateup[:, :ff], gateup[:, ff:])
    sig = sigmoid(gate)
    silu = gate * sig
    act = (silu * up).astype(BF16)
    act_out[...] = act
    grad_gate = grad_hidden * up * (sig * (1.0 + gate * (1.0 - sig)))
    grad = jnp.concatenate([grad_gate, grad_hidden * silu], axis=1).astype(BF16)
    grad_out[...] = grad
    back_out[...] = product_nt(grad, gateup_w).astype(BF16)
    forward_out[...] = product_nt(act, down_w).astype(BF16)


def call(kernel, grid, ins, outs, scratch=()):
    def spec(shape, block, index):
        if block == "smem":
            return pl.BlockSpec(memory_space=pltpu.SMEM)
        if block is None:
            return pl.BlockSpec(shape, lambda i: (0,) * len(shape))
        return pl.BlockSpec(block, index)

    return pl.pallas_call(
        kernel,
        grid=(grid,),
        in_specs=[spec(a.shape, block, index) for a, block, index in ins],
        out_specs=[spec(shape, block, index) for shape, _, block, index in outs],
        out_shape=[jax.ShapeDtypeStruct(shape, kind) for shape, kind, _, _ in outs],
        scratch_shapes=list(scratch),
        compiler_params=pltpu.CompilerParams(
            dimension_semantics=("arbitrary",), vmem_limit_bytes=VMEM_BYTES
        ),
    )(*[a for a, _, _ in ins])


def by_row(i):
    return (i, 0)


def exchange(values, axis, step):
    return lax.ppermute(values, axis, [(k, k ^ step) for k in range(lax.axis_size(axis))])


def bits_of(axis):
    return (lax.axis_size(axis) - 1).bit_length()


def bit_of(axis, bit):
    return (lax.axis_index(axis) >> bit) & 1


def halved(values, axis, at, bit):
    shape = values.shape
    values = values.reshape(shape[:at] + (shape[at] // 2, 2) + shape[at + 1 :])
    mine = bit_of(axis, bit)
    kept = lax.dynamic_index_in_dim(values, mine, at + 1, False)
    sent = lax.dynamic_index_in_dim(values, 1 - mine, at + 1, False)
    return (kept.astype(F32) + exchange(sent, axis, 1 << bit).astype(F32)).astype(BF16)


def scattered(values, axis, at, first_bit=0):
    for bit in range(first_bit, bits_of(axis)):
        values = halved(values, axis, at, bit)
    return lax.squeeze(values, (at,))


def gathered(values, axis):
    bits = bits_of(axis)
    for place, bit in enumerate(reversed(range(bits))):
        other = exchange(values, axis, 1 << bit)
        upper = bit_of(axis, bit) == 1
        values = jnp.stack(
            [jnp.where(upper, other, values), jnp.where(upper, values, other)], axis=place
        )
    shape = values.shape[bits:]
    return values.reshape((lax.axis_size(axis),) + shape)


def summed_over(values, axes):
    for axis in axes:
        for bit in range(bits_of(axis)):
            values = values + exchange(values, axis, 1 << bit)
    return values


class Owned:
    def __init__(self, terms, along):
        dp, ctx = (lax.axis_size(name) for name in WEIGHT_AXES)
        rows, columns = terms.shape
        self.shape = (rows // (dp * ctx), columns)
        self.values = terms.astype(BF16).reshape((dp, ctx) + self.shape)
        over_ctx = [("ctx", 1, bit) for bit in range(bits_of("ctx"))]
        over_dp = [("dp", 0, bit) for bit in range(bits_of("dp"))]
        self.steps = over_ctx + over_dp if along == "ctx" else over_dp + over_ctx

    def step(self):
        if self.steps:
            self.values = halved(self.values, *self.steps.pop(0))

    def result(self):
        while self.steps:
            self.step()
        return self.values.reshape(self.shape).astype(F32)


def in_order(owned, *others):
    values, others = lax.optimization_barrier(([one.values for one in owned], others))
    for one, value in zip(owned, values):
        one.values = value
    return others


def chain(gathered, order, width, heads, reached):
    state = jnp.zeros((width, NST), F32)
    for k in order:
        own = gathered[k, :width].astype(F32)
        through = gathered[k, width].astype(F32) + gathered[k, width + 1].astype(F32)
        wide = jnp.repeat(through[:heads], PD)[:, None]
        state = jnp.where(reached(k), wide * state + own, state)
    return state


def rms_scale(values, gain):
    return values * lax.rsqrt(jnp.mean(values * values, axis=-1, keepdims=True) + EPS) * gain


def rms_back(values, gain, grad):
    scale = lax.rsqrt(jnp.mean(values * values, axis=-1, keepdims=True) + EPS)
    unit = values * scale
    inner = jnp.mean(grad * gain * values, axis=-1, keepdims=True)
    return (scale * (grad * gain - values * scale * scale * inner), jnp.sum(grad * unit, axis=0))


def body(
    tokens,
    cotangent,
    lengths,
    norm1_gain,
    norm2_gain,
    query_proj,
    keyval_proj,
    attn_proj,
    inner_proj,
    state_proj,
    step_proj,
    conv_inner,
    conv_state,
    step_bias,
    decay_log,
    skip_gain,
    mamba_gain,
    mamba_proj,
    gateup_proj,
    down_proj,
):
    rows = tokens.shape[0]
    rank = lax.axis_index("tp")
    ranks = lax.axis_size("tp")
    ctx_rank = lax.axis_index("ctx")
    ctx_size = lax.axis_size("ctx")
    pack = rows * ctx_size
    shard = query_proj.shape[0]
    width = inner_proj.shape[2]
    heads = width // PD
    mix = width + 2 * NST
    ff = gateup_proj.shape[2]
    docs = lengths.shape[1]
    quarter = rows // ranks
    chunks = rows // CHUNK
    kv_head = rank * (query_proj.shape[1] // HD) // (H // KVH)

    kv_shard = lax.dynamic_slice_in_dim(keyval_proj, kv_head * HD, HD, 2).reshape(shard, 2 * HD)
    step_shard = jnp.pad(step_proj, ((0, 0), (0, LANES - heads)))
    inner_shard = inner_proj.reshape(shard, 2 * width)
    first_shard = jnp.concatenate(
        [inner_shard[:, width:], state_proj.reshape(shard, 2 * NST), query_proj, kv_shard, step_shard],
        axis=1,
    )
    mixer_shard = jnp.concatenate([inner_shard[:, :width], attn_proj.T, mamba_proj.T], axis=1)
    last_shard = jnp.concatenate([gateup_proj.reshape(shard, 2 * ff), down_proj.T], axis=1)

    def whole(part):
        return lax.all_gather(part, WEIGHT_AXES, axis=0, tiled=True)

    first_w = whole(first_shard)
    second_w = whole(mixer_shard)
    gate_w = second_w[:, :width]
    mixer_w = second_w[:, width:]
    last_w = whole(last_shard)

    first_row = ctx_rank * rows
    bounds = jnp.cumsum(lengths[0])
    starts = bounds - lengths[0] - first_row
    meta = jnp.concatenate([starts, first_row[None]]).astype(jnp.int32)
    local = jnp.arange(rows, dtype=jnp.int32)
    doc_start = jnp.max(
        jnp.where(local[:, None] >= starts[None, :], starts[None, :], starts[0]), axis=1
    )
    frequency = ROPE_BASE ** (-jnp.arange(HD // 2, dtype=F32) / (HD // 2))
    angles = (local - doc_start).astype(F32)[:, None] * jnp.tile(frequency, 4)[None, :]
    sign = jnp.where(jnp.arange(LANES) % HD < HD // 2, -1.0, 1.0).astype(F32)
    cosine = jnp.cos(angles)
    sine = jnp.sin(angles) * sign[None, :]

    def mine(values, size, axis):
        return lax.dynamic_slice_in_dim(values, rank * size, size, axis)

    taps = jnp.concatenate([mine(conv_inner, width, 1), conv_state.reshape(CONV + 1, -1)], axis=1)
    taps = jnp.pad(taps, ((0, 8 - (CONV + 1)), (0, 0)))
    bias = mine(step_bias, heads, 0)
    rate = jnp.exp(mine(decay_log, heads, 0))
    head_params = jnp.pad(jnp.stack([bias, rate]), ((0, 6), (0, LANES - heads)))
    params = jnp.pad(
        jnp.stack([jnp.repeat(mine(skip_gain, heads, 0), PD), mine(mamba_gain, width, 0)]),
        ((0, 6), (0, 0)),
    )
    channel_head = jnp.arange(width) // PD
    spread = (jnp.arange(LANES)[:, None] == channel_head[None, :]).astype(BF16)
    spread_t = spread.T
    block_ones = (channel_head[:, None] == channel_head[None, :]).astype(BF16)

    normed = lax.optimization_barrier(rms_scale(tokens.astype(F32), norm1_gain).astype(BF16))
    onward = [(source, source + 1) for source in range(ctx_size - 1)]
    backward = [(source + 1, source) for source in range(ctx_size - 1)]
    edge_tokens = lax.ppermute(tokens[rows - EDGE :], "ctx", onward).astype(F32)
    edge_normed = rms_scale(edge_tokens, norm1_gain).astype(BF16)
    proj = product(normed, first_w)
    edge = product(edge_normed, first_w[:, :mix]).astype(BF16).astype(F32)

    chunk_128 = (CHUNK, LANES)
    chunk_mix = (CHUNK, mix)
    chunk_width = (CHUNK, width)
    q_rot, kv_local, mixed, act, slope, step, sig, cum, state_local, end = call(
        functools.partial(prep_kernel, docs, width),
        chunks,
        [
            (meta, "smem", None),
            (proj, (CHUNK, proj.shape[1]), by_row),
            (edge, None, None),
            (taps, None, None),
            (head_params, None, None),
            (cosine, chunk_128, by_row),
            (sine, chunk_128, by_row),
            (spread, None, None),
            (spread_t, None, None),
        ],
        [
            ((rows, LANES), BF16, chunk_128, by_row),
            ((rows, LANES), BF16, chunk_128, by_row),
            ((rows, mix), BF16, chunk_mix, by_row),
            ((rows, mix), F32, chunk_mix, by_row),
            ((rows, mix), F32, chunk_mix, by_row),
            ((rows, LANES), F32, chunk_128, by_row),
            ((rows, LANES), F32, chunk_128, by_row),
            ((rows, LANES), F32, chunk_128, by_row),
            ((chunks * width, NST), F32, (width, NST), by_row),
            ((width + 16, NST), BF16, None, None),
        ],
        [
            pltpu.VMEM((CHUNK + EDGE, mix), F32),
            pltpu.VMEM((width, NST), F32),
            pltpu.VMEM((8, LANES), F32),
        ],
    )
    ends = gathered(end, "ctx")
    kv_all = gathered(kv_local, "ctx").reshape(pack, LANES)
    (y_intra,) = call(
        functools.partial(intra_kernel, docs, width),
        chunks,
        [
            (meta, "smem", None),
            (act, chunk_mix, by_row),
            (step, chunk_128, by_row),
            (cum, chunk_128, by_row),
            (spread, None, None),
        ],
        [((rows, width), F32, chunk_width, by_row)],
    )
    blocks = rows // QUERY_BLOCK
    block_128 = (QUERY_BLOCK, LANES)
    attended, lse = call(
        functools.partial(attend_kernel, docs),
        blocks,
        [(meta, "smem", None), (q_rot, block_128, by_row), (kv_all, None, None)],
        [((rows, LANES), BF16, block_128, by_row), ((rows, LANES), F32, block_128, by_row)],
    )
    normed_again, _ = lax.optimization_barrier((normed, (attended, y_intra)))
    gate_z = product(normed_again, gate_w)
    state_in = chain(ends, range(ctx_size - 1), width, heads, lambda k: k < ctx_rank)
    mixer_low, y, states = call(
        functools.partial(finish_kernel, docs, width),
        chunks,
        [
            (meta, "smem", None),
            (y_intra, chunk_width, by_row),
            (act, chunk_mix, by_row),
            (cum, chunk_128, by_row),
            (gate_z, chunk_width, by_row),
            (attended, chunk_128, by_row),
            (state_local, (width, NST), by_row),
            (state_in, None, None),
            (params, None, None),
            (spread, None, None),
            (spread_t, None, None),
            (block_ones, None, None),
        ],
        [
            ((rows, LANES + width), BF16, (CHUNK, LANES + width), by_row),
            ((rows, width), F32, chunk_width, by_row),
            ((chunks * width, NST), F32, (width, NST), by_row),
        ],
        [pltpu.VMEM((width, NST), F32)],
    )

    def scatter_rows(values, first_after=(), then_after=()):
        values, _ = lax.optimization_barrier((values, first_after))
        values = values.reshape(ranks, quarter, values.shape[1])
        values = halved(values, "tp", 0, 0)
        values, _ = lax.optimization_barrier((values, then_after))
        return scattered(values, "tp", 0, 1).astype(F32)

    def scatter_product(left, right):
        halves = left.reshape(ranks // 2, 2, quarter, left.shape[1])

        def half(which):
            chosen = lax.dynamic_index_in_dim(halves, which, 1, False)
            return product_nt(chosen.reshape(-1, left.shape[1]), right).astype(BF16)

        bit = bit_of("tp", 0)
        sent, kept = lax.optimization_barrier((half(1 - bit), half(bit)))
        values = kept.astype(F32) + exchange(sent, "tp", 1).astype(F32)
        values = values.astype(BF16).reshape(ranks // 2, quarter, right.shape[0])
        return scattered(values, "tp", 0, 1).astype(F32)

    def row_major(values):
        return with_layout_constraint(values, Layout(major_to_minor=(0, 1)))

    def gather_rows(values):
        return gathered(values, "tp").reshape(rows, values.shape[1])

    hidden_q = mine(tokens, quarter, 0).astype(F32)
    residual = hidden_q + scatter_product(mixer_low, mixer_w)
    normed2 = gather_rows(rms_scale(residual, norm2_gain).astype(BF16))
    row_block = (CHUNK, tokens.shape[1])
    hidden_act, grad_gateup, back_part, forward_part = call(
        functools.partial(feed_kernel, ff),
        chunks,
        [
            (normed2, row_block, by_row),
            (cotangent, row_block, by_row),
            (last_w, None, None),
        ],
        [
            ((rows, ff), BF16, (CHUNK, ff), by_row),
            ((rows, 2 * ff), BF16, (CHUNK, 2 * ff), by_row),
            (tokens.shape, BF16, row_block, by_row),
            (tokens.shape, BF16, row_block, by_row),
        ],
    )
    grad_norm2 = scatter_rows(back_part)
    grad_values, norm2_part = rms_back(residual, norm2_gain, grad_norm2)
    grad_residual = mine(cotangent, quarter, 0).astype(F32) + grad_values
    late_terms = row_major(
        jnp.concatenate(
            [
                product_tn(normed2, grad_gateup).astype(BF16),
                product_tn(cotangent, hidden_act).astype(BF16),
            ],
            axis=1,
        )
    )
    grad_residual, late_terms = lax.optimization_barrier((grad_residual, late_terms))
    late_grad = lax.psum_scatter(
        late_terms, WEIGHT_AXES, scatter_dimension=0, tiled=True
    ).astype(F32)
    gateup_grad = late_grad[:, : 2 * ff].reshape(gateup_proj.shape)
    down_grad = late_grad[:, 2 * ff :].T
    grad_mix = gather_rows(grad_residual.astype(BF16))
    layer_half = scatter_rows(forward_part, grad_residual, grad_mix)
    layer_q = (residual + layer_half).astype(BF16)

    grad_mixer = product(grad_mix, mixer_w)
    mixer_terms = product_tn(grad_mix, mixer_low).astype(BF16)
    grad_att = grad_mixer[:, :LANES]
    grad_mamba = grad_mixer[:, LANES:]
    grad_y, grad_gate, params_grad, grad_in = call(
        functools.partial(finish_back_kernel, docs, width),
        chunks,
        [
            (meta, "smem", None),
            (grad_mamba, chunk_width, by_row),
            (y, chunk_width, by_row),
            (act, chunk_mix, by_row),
            (cum, chunk_128, by_row),
            (gate_z, chunk_width, by_row),
            (params, None, None),
            (spread, None, None),
            (block_ones, None, None),
        ],
        [
            ((rows, width), F32, chunk_width, by_row),
            ((rows, width), BF16, chunk_width, by_row),
            ((8, width), F32, None, None),
            ((width, NST), F32, None, None),
        ],
        [pltpu.VMEM((8, LANES), F32)],
    )
    grad_ins = gathered(jnp.concatenate([grad_in.astype(BF16), end[width:]], axis=0), "ctx")
    grad_query, grad_kv = call(
        functools.partial(attend_back_kernel, docs),
        blocks,
        [
            (meta, "smem", None),
            (q_rot, block_128, by_row),
            (kv_all, None, None),
            (grad_att, block_128, by_row),
            (attended, block_128, by_row),
            (lse, block_128, by_row),
            (cosine, block_128, by_row),
            (sine, block_128, by_row),
        ],
        [
            ((rows, LANES), BF16, block_128, by_row),
            ((pack, LANES), F32, None, None),
        ],
    )
    grad_kv = scattered(
        grad_kv.astype(BF16).reshape(ctx_size, rows, LANES), "ctx", 0
    ).astype(F32)
    half = HD // 2
    swapped = jnp.concatenate([grad_kv[:, half:HD], grad_kv[:, :half], grad_kv[:, HD:]], axis=1)
    is_key = jnp.arange(LANES)[None, :] < HD
    grad_kv = jnp.where(is_key, grad_kv * cosine - swapped * sine, grad_kv).astype(BF16)
    grad_end = chain(
        grad_ins, range(ctx_size - 1, 0, -1), width, heads, lambda k: k > ctx_rank
    )
    gate_terms = product_tn(normed, jnp.concatenate([grad_gate, grad_query], axis=1)).astype(BF16)
    second_terms = row_major(jnp.concatenate([mixer_terms, gate_terms], axis=1))
    second_terms, grad_end, layer_q = lax.optimization_barrier((second_terms, grad_end, layer_q))
    second_grad = lax.psum_scatter(
        second_terms, WEIGHT_AXES, scatter_dimension=0, tiled=True
    ).astype(F32)
    attn_grad = second_grad[:, :LANES].T
    mamba_grad = second_grad[:, LANES : LANES + width].T
    query_grad = second_grad[:, LANES + 2 * width :]
    layer_out = gather_rows(layer_q)

    def back_row(i):
        return (chunks - 1 - i, 0)

    grad_mixed, grad_step, grad_tail, grad_edge, taps_grad, heads_grad = call(
        functools.partial(scan_back_kernel, docs, width),
        chunks,
        [
            (meta, "smem", None),
            (act, chunk_mix, back_row),
            (slope, chunk_mix, back_row),
            (step, chunk_128, back_row),
            (sig, chunk_128, back_row),
            (cum, chunk_128, back_row),
            (grad_y, chunk_width, back_row),
            (states, (width, NST), back_row),
            (grad_end, None, None),
            (mixed, chunk_mix, back_row),
            (edge, None, None),
            (taps, None, None),
            (head_params, None, None),
            (params, None, None),
            (spread, None, None),
            (spread_t, None, None),
        ],
        [
            ((rows, mix), BF16, chunk_mix, back_row),
            ((rows, LANES), BF16, chunk_128, back_row),
            ((EDGE, mix), F32, None, None),
            ((EDGE, mix), F32, None, None),
            ((8, mix), F32, None, None),
            ((8, LANES), F32, None, None),
        ],
        [pltpu.VMEM((CHUNK + 2 * EDGE, mix), F32), pltpu.VMEM((width, NST), F32)],
    )
    edge_grad = lax.ppermute(grad_edge, "ctx", backward)
    grad_mixed = lax.dynamic_update_slice_in_dim(
        grad_mixed, (grad_tail + edge_grad).astype(BF16), rows - EDGE, 0
    )
    mixed_a = grad_mixed[:, : width + NST]
    mixed_b = jnp.concatenate([grad_mixed[:, width + NST :], grad_kv, grad_step], axis=1)
    late_a = Owned(product_tn(normed, mixed_a), "ctx")
    late_b = Owned(product_tn(normed, mixed_b), "dp")
    grad_all = jnp.concatenate([grad_mixed, grad_query, grad_kv, grad_step, grad_gate], axis=1)
    all_w = jnp.concatenate([first_w, gate_w], axis=1)
    (grad_all,) = in_order([late_a, late_b], grad_all)
    late_a.step()
    late_b.step()
    grad_norm1 = scatter_product(grad_all, all_w)
    grad_values, norm1_part = rms_back(hidden_q, norm1_gain, grad_norm1)
    tokens_grad = gather_rows((grad_residual + grad_values).astype(BF16))
    owned_a = late_a.result()
    owned_b = late_b.result()
    inner_grad = jnp.concatenate(
        [second_grad[:, LANES + width : LANES + 2 * width], owned_a[:, :width]], axis=1
    ).reshape(inner_proj.shape)
    kv_owned = owned_b[:, NST : NST + LANES]
    step_grad = owned_b[:, NST + LANES : NST + LANES + heads]
    kv_wide = lax.dynamic_update_slice_in_dim(
        jnp.zeros(keyval_proj.shape, F32), kv_owned.reshape(shard, 2, HD), kv_head * HD, 2
    )
    shared = jnp.concatenate(
        [kv_wide.reshape(shard, -1), owned_a[:, width:], owned_b[:, :NST]], axis=1
    ).astype(BF16)
    for bit in range(bits_of("tp")):
        other = exchange(shared, "tp", 1 << bit).astype(F32)
        shared = shared.astype(F32) + other
        if bit + 1 < bits_of("tp"):
            shared = shared.astype(BF16)
    keyval_grad = shared[:, : 2 * KVH * HD].reshape(keyval_proj.shape)
    state_grad = shared[:, 2 * KVH * HD :].reshape(state_proj.shape)

    norms = jnp.concatenate([norm1_part.reshape(8, -1), norm2_part.reshape(8, -1)], axis=1)
    small = jnp.concatenate([taps_grad, heads_grad, params_grad, norms], axis=1)
    small = gathered(summed_over(small, ("ctx", "dp")), "tp")
    at = mix + LANES
    convin_grad = small[:, : CONV + 1, :width].transpose(1, 0, 2).reshape(conv_inner.shape)
    stepbias_grad = small[:, 0, mix : mix + heads].reshape(-1)
    decay_grad = small[:, 1, mix : mix + heads].reshape(-1)
    skip_grad = jnp.sum(small[:, 0, at : at + width].reshape(ranks * heads, PD), axis=1)
    mgain_grad = small[:, 1, at : at + width].reshape(-1)
    shared_small = jnp.sum(small, axis=0)
    convst_grad = shared_small[: CONV + 1, width:mix].reshape(conv_state.shape)
    at = at + width
    norm_columns = norm1_part.shape[0] // 8
    norm1_grad = shared_small[:, at : at + norm_columns].reshape(-1)
    norm2_grad = shared_small[:, at + norm_columns :].reshape(-1)
    return (
        layer_out,
        tokens_grad,
        norm1_grad,
        norm2_grad,
        query_grad,
        keyval_grad,
        attn_grad,
        inner_grad,
        state_grad,
        step_grad,
        convin_grad,
        convst_grad,
        stepbias_grad,
        decay_grad,
        skip_grad,
        mgain_grad,
        mamba_grad,
        gateup_grad,
        down_grad,
    )


def solution(mesh):
    rows_split = P(("dp", "ctx"), None)
    split_0 = P(("dp", "ctx"), "tp")
    split_0_whole = P(("dp", "ctx"), None, None)
    split_0_last = P(("dp", "ctx"), None, "tp")
    split_1 = P("tp", ("dp", "ctx"))
    return jax.shard_map(
        body,
        mesh=mesh,
        in_specs=(
            rows_split,
            rows_split,
            P("dp", None),
            P(),
            P(),
            split_0,
            split_0_whole,
            split_1,
            split_0_last,
            split_0_whole,
            split_0,
            P(),
            P(),
            P(),
            P(),
            P(),
            P(),
            split_1,
            split_0_last,
            split_1,
        ),
        out_specs=(
            rows_split,
            rows_split,
            P(),
            P(),
            split_0,
            split_0_whole,
            split_1,
            split_0_last,
            split_0_whole,
            split_0,
            P(),
            P(),
            P(),
            P(),
            P(),
            P(),
            split_1,
            split_0_last,
            split_1,
        ),
        check_vma=False,
    )
```

profile of v0, /device:TPU:0, one launch (start us, length us, event | category | flops | bytes accessed | tf_op | source)
XLA Modules:
  0.0 432.4 jit_solution(13733891425552541076)
XLA Ops:
  14.5 4.8 %collective-permute-start = (bf16[8,1024]{1,0:T(8,128)(2,1)S(1)}, bf16[8,1024]{1,0:T(8,128)(2,1)S(1)}, u32[]{:S(2)}, u32[]{:S(2)}) collective-permute-start(bf16[8,1024]{1,0:T(8,128)(2,1)S(1)} %slice.140), channel_id=1, source_target_pairs={{0,4},{1,5},{2,6},{3,7},{8,12},{9,13},{10,14},{11,15},{16,20},{17,... | collective-permute-start | bytes 49160 | tf_op jit(solution)/shard_map/ppermute | solution.py:805
  29.2 37.4 %all-gather.4.cloned.1.call-done = bf16[1024,1024]{0,1:T(8,128)(2,1)} async-done(((bf16[128,1024]{0,1:T(8,128)(2,1)}), bf16[1024,1024]{0,1:T(8,128)(2,1)}) %all-gather.4.cloned.1.call-update) | async-done | bytes 2097168 | tf_op jit(solution)/shard_map/all_gather | solution.py:763
  66.6 6.7 %fusion.101.proj = f32[1024,1024]{1,0:T(8,128)} fusion(bf16[1024,1024]{1,0:T(8,128)(2,1)} %fusion.2, bf16[1024,1024]{0,1:T(8,128)(2,1)} %all-gather.4.cloned.1.call-done), kind=kOutput, calls=%fused_computation.268 | convolution fusion | flops 2147483648 | bytes 8388608 | tf_op jit(solution)/shard_map/dot_general | solution.py:34
  73.8 11.1 %shard_map.339 = (bf16[1024,128]{1,0:T(8,128)(2,1)S(1)}, bf16[1024,128]{1,0:T(8,128)(2,1)S(1)}, bf16[1024,640]{1,0:T(8,128)(2,1)S(1)}, f32[1024,640]{1,0:T(8,128...) custom-call(s32[5]{0:T(128)S(1)} %pad_add_fusion.meta, ...), custom_call_target="tpu_custom_call" | custom-call | tf_op jit(solution)/shard_map/pallas_call | solution.py:603
  101.1 6.1 %shard_map.341 = (bf16[1024,128]{1,0:T(8,128)(2,1)S(1)}, f32[1024,128]{1,0:T(8,128)S(1)}) custom-call(s32[5]{0:T(128)S(1)} %pad_add_fusion.meta, bf16[1024,128]{1,0:T(8,128)(2,1)S(1)} %copy-done.13, bf16[2048,128]{1,0:T(8,128)(2,1)S(1)} %bitcast.228), custom_call_target="tpu_custom_call" | custom-call | tf_op jit(solution)/shard_map/pallas_call | solution.py:603
  108.1 7.3 %all-gather.6.cloned.1.call-done = bf16[1024,896]{0,1:T(8,128)(2,1)} async-done(((bf16[128,896]{0,1:T(8,128)(2,1)}), bf16[1024,896]{0,1:T(8,128)(2,1)}) %all-gather.6.cloned.1.call-update) | async-done | bytes 1835024 | tf_op jit(solution)/shard_map/all_gather | solution.py:763
  115.4 4.3 fusion.91.gate
  119.7 5.1 %shard_map.342 = (bf16[1024,512]{1,0:T(8,128)(2,1)S(1)}, f32[1024,384]{1,0:T(8,128)S(1)}, f32[1536,128]{1,0:T(8,128)S(1)}) custom-call(s32[5]{0:T(128)S(1)} %pad_add_fusion.meta, f32[1024,384]{1,0:T(8,128)} %copy-done.3, f32[1024,640]{1,0:T(8,128)} %get-tuple-element.65.act, f32[1024,128]{1,0:T(8,128)S(1)} %get-tuple-element.67.cum, ...), custom_call_target="tpu_custom_call" | custom-call | tf_op jit(solution)/shard_map/pallas_call | solution.py:603
  139.2 12.8 %collective-permute-done.4 = bf16[1,256,1024]{2,1,0:T(8,128)(2,1)} collective-permute-done((bf16[1,256,1024]{2,1,0:T(8,128)(2,1)}, bf16[1,256,1024]{2,1,0:T(8,128)(2,1)}, u32[]{:S(2)}, u32[]{:S(2)}) %collective-permute-start.4) | collective-permute-done | bytes 524320 | tf_op jit(solution)/shard_map/ppermute | solution.py:621
  158.0 12.0 %collective-permute-done.5 = bf16[256,1024]{1,0:T(8,128)(2,1)} collective-permute-done((bf16[256,1024]{1,0:T(8,128)(2,1)}, bf16[256,1024]{1,0:T(8,128)(2,1)}, u32[]{:S(2)}, u32[]{:S(2)}) %collective-permute-start.5) | collective-permute-done | bytes 524320 | tf_op jit(solution)/shard_map/ppermute | solution.py:621
  179.5 11.2 %shard_map.343 = (bf16[1024,512]{1,0:T(8,128)(2,1)S(1)}, bf16[1024,1024]{1,0:T(8,128)(2,1)S(1)}, bf16[1024,1024]{1,0:T(8,128)(2,1)S(1)}, bf16[1024,1024]{1,0:T(8,128)(2,1)}) custom-call(bf16[1024,1024]{1,0:T(8,128)(2,1)} %bitcast.233, bf16[1024,1024]{1,0:T(8,128)(2,1)} %cotangent.1, bf16[1024,1536]{1,0:T(8,128)(2,1)} %all-gather.8.cloned.1.call-done.weights), custom_call_target="tpu_custom_call" | custom-call | tf_op jit(solution)/shard_map/pallas_call | solution.py:603
  200.7 9.6 %collective-permute-done.8 = bf16[1,256,1024]{2,1,0:T(8,128)(2,1)} collective-permute-done((bf16[1,256,1024]{2,1,0:T(8,128)(2,1)}, bf16[1,256,1024]{2,1,0:T(8,128)(2,1)}, u32[]{:S(2)}, u32[]{:S(2)}) %collective-permute-start.8) | collective-permute-done | bytes 524320 | tf_op jit(solution)/shard_map/ppermute | solution.py:621
  217.5 10.6 %collective-permute-done.9 = bf16[256,1024]{1,0:T(8,128)(2,1)S(1)} collective-permute-done((bf16[256,1024]{1,0:T(8,128)(2,1)S(1)}, bf16[256,1024]{1,0:T(8,128)(2,1)S(1)}, u32[]{:S(2)}, u32[]{:S(2)}) %collective-permute-start.9) | collective-permute-done | bytes 524320 | tf_op jit(solution)/shard_map/ppermute | solution.py:621
  241.2 6.5 %shard_map.344 = (f32[1024,384]{1,0:T(8,128)S(1)}, bf16[1024,384]{1,0:T(8,128)(2,1)S(1)}, f32[8,384]{1,0:T(8,128)S(1)}, f32[384,128]{1,0:T(8,128)S(1)}) custom-call(s32[5]{0:T(128)S(1)} %pad_add_fusion.meta, f32[1024,384]{1,0:T(8,128)S(1)} %slice.192.grad, f32[1024,384]{1,0:T(8,128)} %copy-done.4, f32[1024,640]{1,0:T(8,128)} %get-tuple-element.65.act, ...), custom_call_target="tpu_custom_call" | custom-call | tf_op jit(solution)/shard_map/pallas_call | solution.py:603
  251.0 9.3 %shard_map.345 = (bf16[1024,128]{1,0:T(8,128)(2,1)S(1)}, f32[2048,128]{1,0:T(8,128)S(1)}) custom-call(s32[5]{0:T(128)S(1)} %pad_add_fusion.meta, bf16[1024,128]{1,0:T(8,128)(2,1)S(1)} %copy-done.14, bf16[2048,128]{1,0:T(8,128)(2,1)S(1)} %bitcast.229, f32[1024,128]{1,0:T(8,128)S(1)} %slice.193.grad, bf16[1024,128]{1,0:T(8,128)(2,1)S(1)} %get-tuple-element.70.att, ...), custom_call_target="tpu_custom_call" | custom-call | tf_op jit(solution)/shard_map/pallas_call | solution.py:603
  268.4 8.3 %collective-permute-start.17 = (bf16[1,1024,128]{2,1,0:T(8,128)(2,1)S(1)}, bf16[1,1024,128]{2,1,0:T(8,128)(2,1)S(1)}, u32[]{:S(2)}, u32[]{:S(2)}) collective-permute-start(bf16[1,1024,128]{2,1,0:T(8,128)(2,1)S(1)} %dynamic-slice_bitcast_fusion.6), channel_id=1, source_target_pairs={{0,4},{4,0},{1,5},{5,1},{2,6},{6,2},{3,7},{7,3},{8,12},{12,8},{9,1... | collective-permute-start | bytes 786440 | tf_op jit(solution)/shard_map/ppermute | solution.py:621
  279.0 5.8 %collective-permute-done.17 = bf16[1,1024,128]{2,1,0:T(8,128)(2,1)S(1)} collective-permute-done((bf16[1,1024,128]{2,1,0:T(8,128)(2,1)S(1)}, bf16[1,1024,128]{2,1,0:T(8,128)(2,1)S(1)}, u32[]{:S(2)}, u32[]{:S(2)}) %collective-permute-start.17) | collective-permute-done | bytes 262176 | tf_op jit(solution)/shard_map/ppermute | solution.py:621
  286.3 16.8 %shard_map.346 = (bf16[1024,640]{1,0:T(8,128)(2,1)S(1)}, bf16[1024,128]{1,0:T(8,128)(2,1)S(1)}, f32[8,640]{1,0:T(8,128)S(1)}, f32[8,640]{1,0:T(8,128)S(1)}, f32[8,640]{1,0:T(8,128)S(1)}, /*index=5*/f32[8,128]{1,0:T(8,128)S(1)}) custom-call(s32[5]{0:T(128)S(1)} %pad_add_fusion.meta, f32[1024,640]{1,0:T(8,128)} %get-tuple-element.65.act, ...), custom_call_target="tpu_custom_call" | custom-call | tf_op jit(solution)/shard_map/pallas_call | solution.py:603
  324.0 15.2 %collective-permute-done.30 = bf16[4,1,128,512]{3,2,0,1:T(8,128)(2,1)S(1)} collective-permute-done((bf16[4,1,128,512]{3,2,0,1:T(8,128)(2,1)S(1)}, bf16[4,1,128,512]{3,2,0,1:T(8,128)(2,1)S(1)}, u32[]{:S(2)}, u32[]{:S(2)}) %collective-permute-start.30) | collective-permute-done | bytes 524320 | tf_op jit(solution)/shard_map/ppermute | solution.py:621
  349.6 7.8 %collective-permute-done.32 = bf16[1,1,128,512]{3,2,1,0:T(8,128)(2,1)S(1)} collective-permute-done((bf16[1,1,128,512]{3,2,1,0:T(8,128)(2,1)S(1)}, bf16[1,1,128,512]{3,2,1,0:T(8,128)(2,1)S(1)}, u32[]{:S(2)}, u32[]{:S(2)}) %collective-permute-start.32) | collective-permute-done | bytes 131104 | tf_op jit(solution)/shard_map/ppermute | solution.py:621
  361.7 14.8 %collective-permute-done.34 = bf16[128,512]{0,1:T(8,128)(2,1)S(1)} collective-permute-done((bf16[128,512]{0,1:T(8,128)(2,1)S(1)}, bf16[128,512]{0,1:T(8,128)(2,1)S(1)}, u32[]{:S(2)}, u32[]{:S(2)}) %collective-permute-start.34) | collective-permute-done | bytes 131104 | tf_op jit(solution)/shard_map/ppermute | solution.py:621
  384.8 4.0 collective-permute-done.23
  395.6 8.2 %collective-permute-done.25 = f32[8,1408]{1,0:T(8,128)S(1)} collective-permute-done((f32[8,1408]{1,0:T(8,128)S(1)}, f32[8,1408]{1,0:T(8,128)S(1)}, u32[]{:S(2)}, u32[]{:S(2)}) %collective-permute-start.25) | collective-permute-done | bytes 45088 | tf_op jit(solution)/shard_map/ppermute | solution.py:621
  417.7 3.7 reduce-scatter.5.cloned.1.call-done
  (430 shorter events, 176.7 us)
Async XLA Ops:
  7.2 59.4 %all-gather.4.cloned.1.call-start = ((), (), s32[]{:S(2)}) async-start(), calls=%async_computation.2 | async-start | bytes 2359296 | tf_op jit(solution)/shard_map/all_gather | solution.py:763
  12.7 102.7 %all-gather.6.cloned.1.call-start = ((), (), s32[]{:S(2)}) async-start(), calls=%async_computation.3 | async-start | bytes 2064384 | tf_op jit(solution)/shard_map/all_gather | solution.py:763
  14.4 165.1 %all-gather.8.cloned.1.call-start = ((), (), s32[]{:S(2)}) async-start(), calls=%async_computation.4 | async-start | bytes 3538944 | tf_op jit(solution)/shard_map/all_gather | solution.py:763
  14.5 14.6 %collective-permute-start = (bf16[8,1024]{1,0:T(8,128)(2,1)S(1)}, bf16[8,1024]{1,0:T(8,128)(2,1)S(1)}, u32[]{:S(2)}, u32[]{:S(2)}) collective-permute-start(bf16[8,1024]{1,0:T(8,128)(2,1)S(1)} %slice.140), channel_id=1, source_target_pairs={{0,4},{1,5},{2,6},{3,7},{8,12},{9,13},{10,14},{11,15},{16,20},{17,... | collective-permute-start | bytes 49160 | tf_op jit(solution)/shard_map/ppermute | solution.py:805
  20.3 393.8 %reduce-scatter.3.cloned.1.call-start = ((), (), s32[]{:S(2)}) async-start(), calls=%async_computation.5 | async-start | bytes 2359296 | tf_op jit(solution)/shard_map/reduce_scatter | solution.py:1020
  89.0 11.1 %collective-permute-start.1 = (bf16[1024,128]{1,0:T(8,128)(2,1)S(1)}, bf16[1024,128]{1,0:T(8,128)(2,1)S(1)}, u32[]{:S(2)}, u32[]{:S(2)}) collective-permute-start(bf16[1024,128]{1,0:T(8,128)(2,1)S(1)} %get-tuple-element.69), channel_id=1, source_target_pairs={{0,4},{4,0},{1,5},{5,1},{2,6},{6,2},{3,7},{7,3},{8,12},{12,8},{9,1... | collective-permute-start | bytes 786440 | tf_op jit(solution)/shard_map/ppermute | solution.py:621
  137.7 14.3 %collective-permute-start.4 = (bf16[1,256,1024]{2,1,0:T(8,128)(2,1)}, bf16[1,256,1024]{2,1,0:T(8,128)(2,1)}, u32[]{:S(2)}, u32[]{:S(2)}) collective-permute-start(bf16[1,256,1024]{2,1,0:T(8,128)(2,1)} %dynamic-slice_bitcast_fusion.3), channel_id=1, source_target_pairs={{0,2},{1,3},{2,0},{3,1},{4,6},{5,7},{6,4},{7,5},{8,10},{9,11},{10,... | collective-permute-start | bytes 1572872 | tf_op jit(solution)/shard_map/ppermute | solution.py:621
  156.6 13.4 %collective-permute-start.5 = (bf16[256,1024]{1,0:T(8,128)(2,1)}, bf16[256,1024]{1,0:T(8,128)(2,1)}, u32[]{:S(2)}, u32[]{:S(2)}) collective-permute-start(bf16[256,1024]{1,0:T(8,128)(2,1)} %multiply_convert_fusion), channel_id=1, source_target_pairs={{0,2},{1,3},{2,0},{3,1},{4,6},{5,7},{6,4},{7,5},{8,10},{9,11},{10,... | collective-permute-start | bytes 1572872 | tf_op jit(solution)/shard_map/ppermute | solution.py:621
  196.0 14.3 %collective-permute-start.8 = (bf16[1,256,1024]{2,1,0:T(8,128)(2,1)}, bf16[1,256,1024]{2,1,0:T(8,128)(2,1)}, u32[]{:S(2)}, u32[]{:S(2)}) collective-permute-start(bf16[1,256,1024]{2,1,0:T(8,128)(2,1)} %constant_dynamic-slice_fusion.7), channel_id=1, source_target_pairs={{0,2},{1,3},{2,0},{3,1},{4,6},{5,7},{6,4},{7,5},{8,10},{9,11},{10,... | collective-permute-start | bytes 1572872 | tf_op jit(solution)/shard_map/ppermute | solution.py:621
  214.9 13.2 %collective-permute-start.9 = (bf16[256,1024]{1,0:T(8,128)(2,1)S(1)}, bf16[256,1024]{1,0:T(8,128)(2,1)S(1)}, u32[]{:S(2)}, u32[]{:S(2)}) collective-permute-start(bf16[256,1024]{1,0:T(8,128)(2,1)S(1)} %convert_element_type.448), channel_id=1, source_target_pairs={{0,2},{1,3},{2,0},{3,1},{4,6},{5,7},{6,4},{7,5},{8,10},{9,11},{10,... | collective-permute-start | bytes 1572872 | tf_op jit(solution)/shard_map/ppermute | solution.py:621
  217.5 12.7 %collective-permute-start.12 = (bf16[2,256,1024]{2,1,0:T(8,128)(2,1)}, bf16[2,256,1024]{2,1,0:T(8,128)(2,1)}, u32[]{:S(2)}, u32[]{:S(2)}) collective-permute-start(bf16[2,256,1024]{2,1,0:T(8,128)(2,1)} %dynamic-slice_bitcast_fusion), channel_id=1, source_target_pairs={{0,1},{1,0},{2,3},{3,2},{4,5},{5,4},{6,7},{7,6},{8,9},{9,8},{10,11... | collective-permute-start | bytes 3145736 | tf_op jit(solution)/shard_map/ppermute | solution.py:621
  239.7 24.9 %collective-permute-start.13 = (bf16[1,256,1024]{2,1,0:T(8,128)(2,1)}, bf16[1,256,1024]{2,1,0:T(8,128)(2,1)}, u32[]{:S(2)}, u32[]{:S(2)}) collective-permute-start(bf16[1,256,1024]{2,1,0:T(8,128)(2,1)} %constant_dynamic-slice_fusion.6), channel_id=1, source_target_pairs={{0,2},{1,3},{2,0},{3,1},{4,6},{5,7},{6,4},{7,5},{8,10},{9,11},{10,... | collective-permute-start | bytes 1572872 | tf_op jit(solution)/shard_map/ppermute | solution.py:621
  249.6 13.8 %collective-permute-start.11 = (bf16[400,128]{1,0:T(8,128)(2,1)}, bf16[400,128]{1,0:T(8,128)(2,1)}, u32[]{:S(2)}, u32[]{:S(2)}) collective-permute-start(bf16[400,128]{1,0:T(8,128)(2,1)} %pad_maximum_fusion.23), channel_id=1, source_target_pairs={{0,4},{4,0},{1,5},{5,1},{2,6},{6,2},{3,7},{7,3},{8,12},{12,8},{9,1... | collective-permute-start | bytes 307208 | tf_op jit(solution)/shard_map/ppermute | solution.py:621
  267.5 154.0 %reduce-scatter.5.cloned.1.call-start = ((), (), s32[]{:S(2)}) async-start(), calls=%async_computation.6 | async-start | bytes 3538944 | tf_op jit(solution)/shard_map/reduce_scatter | solution.py:953
  268.4 16.4 %collective-permute-start.17 = (bf16[1,1024,128]{2,1,0:T(8,128)(2,1)S(1)}, bf16[1,1024,128]{2,1,0:T(8,128)(2,1)S(1)}, u32[]{:S(2)}, u32[]{:S(2)}) collective-permute-start(bf16[1,1024,128]{2,1,0:T(8,128)(2,1)S(1)} %dynamic-slice_bitcast_fusion.6), channel_id=1, source_target_pairs={{0,4},{4,0},{1,5},{5,1},{2,6},{6,2},{3,7},{7,3},{8,12},{12,8},{9,1... | collective-permute-start | bytes 786440 | tf_op jit(solution)/shard_map/ppermute | solution.py:621
  305.2 18.8 %collective-permute-start.14 = (bf16[256,1024]{1,0:T(8,128)(2,1)S(1)}, bf16[256,1024]{1,0:T(8,128)(2,1)S(1)}, u32[]{:S(2)}, u32[]{:S(2)}) collective-permute-start(bf16[256,1024]{1,0:T(8,128)(2,1)S(1)} %copy-done.48), channel_id=1, source_target_pairs={{0,2},{1,3},{2,0},{3,1},{4,6},{5,7},{6,4},{7,5},{8,10},{9,11},{10,... | collective-permute-start | bytes 1572872 | tf_op jit(solution)/shard_map/ppermute | solution.py:621
  322.0 35.7 %collective-permute-start.18 = (bf16[512,1024]{1,0:T(8,128)(2,1)}, bf16[512,1024]{1,0:T(8,128)(2,1)}, u32[]{:S(2)}, u32[]{:S(2)}) collective-permute-start(bf16[512,1024]{1,0:T(8,128)(2,1)} %fusion.7), channel_id=1, source_target_pairs={{0,1},{1,0},{2,3},{3,2},{4,5},{5,4},{6,7},{7,6},{8,9},{9,8},{10,11... | collective-permute-start | bytes 3145736 | tf_op jit(solution)/shard_map/ppermute | solution.py:621
  322.0 17.2 %collective-permute-start.30 = (bf16[4,1,128,512]{3,2,0,1:T(8,128)(2,1)S(1)}, bf16[4,1,128,512]{3,2,0,1:T(8,128)(2,1)S(1)}, u32[]{:S(2)}, u32[]{:S(2)}) collective-permute-start(bf16[4,1,128,512]{3,2,0,1:T(8,128)(2,1)S(1)} %constant_dynamic-slice_fusion.1), channel_id=1, source_target_pairs={{0,4},{4,0},{1,5},{5,1},{2,6},{6,2},{3,7},{7,3},{8,12},{12,8},{9,1... | collective-permute-start | bytes 1572872 | tf_op jit(solution)/shard_map/ppermute | solution.py:621
  323.9 19.0 %collective-permute-start.28 = (bf16[1,2,128,384]{3,2,1,0:T(8,128)(2,1)S(1)}, bf16[1,2,128,384]{3,2,1,0:T(8,128)(2,1)S(1)}, u32[]{:S(2)}, u32[]{:S(2)}) collective-permute-start(bf16[1,2,128,384]{3,2,1,0:T(8,128)(2,1)S(1)} %constant_dynamic-slice_fusion.3), channel_id=1, source_target_pairs={{0,16},{8,24},{16,0},{24,8},{1,17},{9,25},{17,1},{25,9},{2,18},{10... | collective-permute-start | bytes 589832 | tf_op jit(solution)/shard_map/ppermute | solution.py:621
  345.7 48.6 %collective-permute-start.15 = (bf16[2,256,1024]{2,1,0:T(8,128)(2,1)}, bf16[2,256,1024]{2,1,0:T(8,128)(2,1)}, u32[]{:S(2)}, u32[]{:S(2)}) collective-permute-start(bf16[2,256,1024]{2,1,0:T(8,128)(2,1)} %pad_maximum_fusion.15), channel_id=1, source_target_pairs={{0,1},{1,0},{2,3},{3,2},{4,5},{5,4},{6,7},{7,6},{8,9},{9,8},{10,11... | collective-permute-start | bytes 3145736 | tf_op jit(solution)/shard_map/ppermute | solution.py:621
  359.5 17.1 %collective-permute-start.19 = (bf16[1,256,1024]{2,1,0:T(8,128)(2,1)S(1)}, bf16[1,256,1024]{2,1,0:T(8,128)(2,1)S(1)}, u32[]{:S(2)}, u32[]{:S(2)}) collective-permute-start(bf16[1,256,1024]{2,1,0:T(8,128)(2,1)S(1)} %dynamic-slice_bitcast_fusion.2), channel_id=1, source_target_pairs={{0,2},{1,3},{2,0},{3,1},{4,6},{5,7},{6,4},{7,5},{8,10},{9,11},{10,... | collective-permute-start | bytes 1572872 | tf_op jit(solution)/shard_map/ppermute | solution.py:621
  360.4 16.2 %collective-permute-start.34 = (bf16[128,512]{0,1:T(8,128)(2,1)S(1)}, bf16[128,512]{0,1:T(8,128)(2,1)S(1)}, u32[]{:S(2)}, u32[]{:S(2)}) collective-permute-start(bf16[128,512]{0,1:T(8,128)(2,1)S(1)} %add_convert_fusion.6), channel_id=1, source_target_pairs={{0,2},{1,3},{2,0},{3,1},{4,6},{5,7},{6,4},{7,5},{8,10},{9,11},{10,... | collective-permute-start | bytes 393224 | tf_op jit(solution)/shard_map/ppermute | solution.py:621
  390.4 13.5 %collective-permute-start.20 = (bf16[256,1024]{1,0:T(8,128)(2,1)S(1)}, bf16[256,1024]{1,0:T(8,128)(2,1)S(1)}, u32[]{:S(2)}, u32[]{:S(2)}) collective-permute-start(bf16[256,1024]{1,0:T(8,128)(2,1)S(1)} %fusion.28), channel_id=1, source_target_pairs={{0,2},{1,3},{2,0},{3,1},{4,6},{5,7},{6,4},{7,5},{8,10},{9,11},{10,... | collective-permute-start | bytes 1572872 | tf_op jit(solution)/shard_map/ppermute | solution.py:621
  393.9 10.0 %collective-permute-start.25 = (f32[8,1408]{1,0:T(8,128)S(1)}, f32[8,1408]{1,0:T(8,128)S(1)}, u32[]{:S(2)}, u32[]{:S(2)}) collective-permute-start(f32[8,1408]{1,0:T(8,128)S(1)} %add.276), channel_id=1, source_target_pairs={{0,2},{1,3},{2,0},{3,1},{4,6},{5,7},{6,4},{7,5},{8,10},{9,11},{10,... | collective-permute-start | bytes 135176 | tf_op jit(solution)/shard_map/ppermute | solution.py:621
  (94 other events, 533.1 us)
Sparse Core Ops, SparseCore 0:
  12.9 53.7 all-gather.3
  69.3 46.1 all-gather.5
  118.2 59.2 all-gather.7
  267.6 76.3 reduce-scatter.2
  347.4 74.0 reduce-scatter.4
where the time goes:
time: 438 us; the launch traced here: 432 us
  waiting for transfers between devices  173 us (39%)
  Pallas kernels  69.9 us (16%)
  local copies, waits for them, and re-layouts  57 us (13%)
  other arithmetic  52.8 us (12%)
  starting transfers between devices  34.5 us (8%)
  matrix products  29.6 us (7%)
  between operations  15.9 us (4%)
    ppermute x33, waiting for transfers between devices, exchange(): lax.ppermute(values, axis, [(k, k ^ step) for k in range(lax.axis_size(ax...  121 us
    pallas_call x8, Pallas kernels, call(): pl.pallas_call(kernel, grid=(grid,), in_specs=[spec(a.shape, block, index...  69.9 us
    all_gather x3, waiting for transfers between devices, whole(): return lax.all_gather(part, WEIGHT_AXES, axis=0, tiled=True)  44.8 us
    unnamed x178, local copies, waits for them, and re-layouts  32 us
    ppermute x33, starting transfers between devices, exchange(): lax.ppermute(values, axis, [(k, k ^ step) for k in range(lax.axis_size(ax...  28 us
    dot_general x4, matrix products, product(): return jnp.dot(left, right, preferred_element_type=F32)  12.7 us
    another operation x23, other arithmetic, gathered(): jnp.stack([jnp.where(upper, other, values), jnp.where(upper, values, othe...  11.3 us
    dot_general x6, matrix products, product_tn(): lax.dot_general(left, right, (((0,), (0,)), ((), ())), preferred_element_...  8.81 us
  transfers between devices with their start and end apart: 40, of which 24 were waited for; matrix products, arithmetic and copies ran while one was open for 22% of the time, Pallas kernels for 14%

commit v1 on v0

--- a/solution.py
+++ b/solution.py
@@ -594,6 +594,8 @@
 
 def call(kernel, grid, ins, outs, scratch=()):
     def spec(shape, block, index):
+        if block == "any":
+            return pl.BlockSpec(memory_space=pl.ANY)
         if block == "smem":
             return pl.BlockSpec(memory_space=pltpu.SMEM)
         if block is None:
@@ -613,6 +615,21 @@
     )(*[a for a, _, _ in ins])
 
 
+def pass_kernel(*refs):
+    del refs
+
+
+def after(values, *others):
+    anywhere = pl.BlockSpec(memory_space=pl.ANY)
+    return pl.pallas_call(
+        pass_kernel,
+        in_specs=[anywhere] * (1 + len(others)),
+        out_specs=anywhere,
+        out_shape=jax.ShapeDtypeStruct(values.shape, values.dtype),
+        input_output_aliases={0: 0},
+    )(values, *others)
+
+
 def by_row(i):
     return (i, 0)
 
@@ -681,13 +698,6 @@
         while self.steps:
             self.step()
         return self.values.reshape(self.shape).astype(F32)
-
-
-def in_order(owned, *others):
-    values, others = lax.optimization_barrier(([one.values for one in owned], others))
-    for one, value in zip(owned, values):
-        one.values = value
-    return others
 
 
 def chain(gathered, order, width, heads, reached):
@@ -749,7 +759,11 @@
     chunks = rows // CHUNK
     kv_head = rank * (query_proj.shape[1] // HD) // (H // KVH)
 
-    kv_shard = lax.dynamic_slice_in_dim(keyval_proj, kv_head * HD, HD, 2).reshape(shard, 2 * HD)
+    kv_heads = keyval_proj.reshape(shard, 2, KVH, HD)
+    kv_shard = kv_heads[:, :, 0]
+    for head in range(1, KVH):
+        kv_shard = jnp.where(kv_head == head, kv_heads[:, :, head], kv_shard)
+    kv_shard = kv_shard.reshape(shard, 2 * HD)
     step_shard = jnp.pad(step_proj, ((0, 0), (0, LANES - heads)))
     inner_shard = inner_proj.reshape(shard, 2 * width)
     first_shard = jnp.concatenate(
@@ -910,7 +924,7 @@
         sent, kept = lax.optimization_barrier((half(1 - bit), half(bit)))
         values = kept.astype(F32) + exchange(sent, "tp", 1).astype(F32)
         values = values.astype(BF16).reshape(ranks // 2, quarter, right.shape[0])
-        return scattered(values, "tp", 0, 1).astype(F32)
+        return values, lambda: scattered(values, "tp", 0, 1).astype(F32)
 
     def row_major(values):
         return with_layout_constraint(values, Layout(major_to_minor=(0, 1)))
@@ -919,7 +933,7 @@
         return gathered(values, "tp").reshape(rows, values.shape[1])
 
     hidden_q = mine(tokens, quarter, 0).astype(F32)
-    residual = hidden_q + scatter_product(mixer_low, mixer_w)
+    residual = hidden_q + scatter_product(mixer_low, mixer_w)[1]()
     normed2 = gather_rows(rms_scale(residual, norm2_gain).astype(BF16))
     row_block = (CHUNK, tokens.shape[1])
     hidden_act, grad_gateup, back_part, forward_part = call(
@@ -950,11 +964,7 @@
         )
     )
     grad_residual, late_terms = lax.optimization_barrier((grad_residual, late_terms))
-    late_grad = lax.psum_scatter(
-        late_terms, WEIGHT_AXES, scatter_dimension=0, tiled=True
-    ).astype(F32)
-    gateup_grad = late_grad[:, : 2 * ff].reshape(gateup_proj.shape)
-    down_grad = late_grad[:, 2 * ff :].T
+    late_grad = lax.psum_scatter(late_terms, WEIGHT_AXES, scatter_dimension=0, tiled=True)
     grad_mix = gather_rows(grad_residual.astype(BF16))
     layer_half = scatter_rows(forward_part, grad_residual, grad_mix)
     layer_q = (residual + layer_half).astype(BF16)
@@ -1017,12 +1027,7 @@
     gate_terms = product_tn(normed, jnp.concatenate([grad_gate, grad_query], axis=1)).astype(BF16)
     second_terms = row_major(jnp.concatenate([mixer_terms, gate_terms], axis=1))
     second_terms, grad_end, layer_q = lax.optimization_barrier((second_terms, grad_end, layer_q))
-    second_grad = lax.psum_scatter(
-        second_terms, WEIGHT_AXES, scatter_dimension=0, tiled=True
-    ).astype(F32)
-    attn_grad = second_grad[:, :LANES].T
-    mamba_grad = second_grad[:, LANES : LANES + width].T
-    query_grad = second_grad[:, LANES + 2 * width :]
+    second_grad = lax.psum_scatter(second_terms, WEIGHT_AXES, scatter_dimension=0, tiled=True)
     layer_out = gather_rows(layer_q)
 
     def back_row(i):
@@ -1065,29 +1070,35 @@
     )
     mixed_a = grad_mixed[:, : width + NST]
     mixed_b = jnp.concatenate([grad_mixed[:, width + NST :], grad_kv, grad_step], axis=1)
-    late_a = Owned(product_tn(normed, mixed_a), "ctx")
-    late_b = Owned(product_tn(normed, mixed_b), "dp")
     grad_all = jnp.concatenate([grad_mixed, grad_query, grad_kv, grad_step, grad_gate], axis=1)
     all_w = jnp.concatenate([first_w, gate_w], axis=1)
-    (grad_all,) = in_order([late_a, late_b], grad_all)
+    on_chip, finish_rows = scatter_product(grad_all, all_w)
+    late_a = Owned(product_tn(normed, after(mixed_a, on_chip)), "ctx")
+    late_b = Owned(product_tn(normed, after(mixed_b, on_chip)), "dp")
     late_a.step()
     late_b.step()
-    grad_norm1 = scatter_product(grad_all, all_w)
+    grad_norm1 = finish_rows()
     grad_values, norm1_part = rms_back(hidden_q, norm1_gain, grad_norm1)
     tokens_grad = gather_rows((grad_residual + grad_values).astype(BF16))
     owned_a = late_a.result()
     owned_b = late_b.result()
-    inner_grad = jnp.concatenate(
-        [second_grad[:, LANES + width : LANES + 2 * width], owned_a[:, :width]], axis=1
-    ).reshape(inner_proj.shape)
     kv_owned = owned_b[:, NST : NST + LANES]
     step_grad = owned_b[:, NST + LANES : NST + LANES + heads]
-    kv_wide = lax.dynamic_update_slice_in_dim(
-        jnp.zeros(keyval_proj.shape, F32), kv_owned.reshape(shard, 2, HD), kv_head * HD, 2
+    kv_wide = jnp.concatenate(
+        [
+            jnp.where(kv_head == head, kv_owned[:, part * HD : (part + 1) * HD], 0.0)
+            for part in range(2)
+            for head in range(KVH)
+        ],
+        axis=1,
     )
     shared = jnp.concatenate(
-        [kv_wide.reshape(shard, -1), owned_a[:, width:], owned_b[:, :NST]], axis=1
+        [kv_wide, owned_a[:, width:], owned_b[:, :NST]], axis=1
     ).astype(BF16)
+    shared = after(shared, late_grad)
+    late_grad = late_grad.astype(F32)
+    gateup_grad = late_grad[:, : 2 * ff].reshape(gateup_proj.shape)
+    down_grad = late_grad[:, 2 * ff :].T
     for bit in range(bits_of("tp")):
         other = exchange(shared, "tp", 1 << bit).astype(F32)
         shared = shared.astype(F32) + other
@@ -1099,6 +1110,13 @@
     norms = jnp.concatenate([norm1_part.reshape(8, -1), norm2_part.reshape(8, -1)], axis=1)
     small = jnp.concatenate([taps_grad, heads_grad, params_grad, norms], axis=1)
     small = gathered(summed_over(small, ("ctx", "dp")), "tp")
+    second_grad = after(second_grad, shared, tokens_grad, small).astype(F32)
+    attn_grad = second_grad[:, :LANES].T
+    mamba_grad = second_grad[:, LANES : LANES + width].T
+    query_grad = second_grad[:, LANES + 2 * width :]
+    inner_grad = jnp.concatenate(
+        [second_grad[:, LANES + width : LANES + 2 * width], owned_a[:, :width]], axis=1
+    ).reshape(inner_proj.shape)
     at = mix + LANES
     convin_grad = small[:, : CONV + 1, :width].transpose(1, 0, 2).reshape(conv_inner.shape)
     stepbias_grad = small[:, 0, mix : mix + heads].reshape(-1)

time: 438 us -> 429 us (0.979)
  waiting for transfers between devices: 173 us -> 152 us
  other arithmetic: 52.8 us -> 59.4 us
  matrix products: 29.6 us -> 34.4 us
    ppermute x33, waiting for transfers between devices: 121 us -> 105 us  [exchange(): lax.ppermute(values, axis, [(k, k ^ step) for k in range(lax.axis_size(ax...]
    another operation x23, other arithmetic: 11.3 us -> 16 us  [gathered(): jnp.stack([jnp.where(upper, other, values), jnp.where(upper, values, othe...]
    unnamed x178 -> x163, local copies, waits for them, and re-layouts: 32 us -> 30.3 us
  transfers between devices with their start and end apart: 40 -> 40, of which waited for: 24 -> 18; matrix products, arithmetic and copies ran while one was open for 22% -> 26% of each run, Pallas kernels for 14% -> 14%
where the time goes in v1:
time: 429 us; the launch traced here: 422 us
  waiting for transfers between devices  152 us (35%)
  Pallas kernels  70 us (16%)
  other arithmetic  59.4 us (14%)
  local copies, waits for them, and re-layouts  57.4 us (13%)
  matrix products  34.4 us (8%)
  starting transfers between devices  33 us (8%)
  between operations  15.8 us (4%)
    ppermute x33, waiting for transfers between devices, exchange(): lax.ppermute(values, axis, [(k, k ^ step) for k in range(lax.axis_size(ax...  105 us
    pallas_call x8, Pallas kernels, call(): pl.pallas_call(kernel, grid=(grid,), in_specs=[spec(a.shape, block, index...  70 us
    all_gather x3, waiting for transfers between devices, whole(): return lax.all_gather(part, WEIGHT_AXES, axis=0, tiled=True)  45.3 us
    unnamed x163, local copies, waits for them, and re-layouts  30.3 us
    ppermute x33, starting transfers between devices, exchange(): lax.ppermute(values, axis, [(k, k ^ step) for k in range(lax.axis_size(ax...  26.7 us
    another operation x23, other arithmetic, gathered(): jnp.stack([jnp.where(upper, other, values), jnp.where(upper, values, othe...  16 us
    dot_general x4, matrix products, product(): return jnp.dot(left, right, preferred_element_type=F32)  12.8 us
    dot_general x6, matrix products, product_tn(): lax.dot_general(left, right, (((0,), (0,)), ((), ())), preferred_element_...  12.6 us
  transfers between devices with their start and end apart: 40, of which 18 were waited for; matrix products, arithmetic and copies ran while one was open for 26% of the time, Pallas kernels for 14%

profile of v1, /device:TPU:0, one launch (start us, length us, event | category | flops | bytes accessed | tf_op | source)
XLA Modules:
  0.0 422.4 jit_solution(8798228351981379369)
XLA Ops:
  14.6 4.8 %collective-permute-start = (bf16[8,1024]{1,0:T(8,128)(2,1)S(1)}, bf16[8,1024]{1,0:T(8,128)(2,1)S(1)}, u32[]{:S(2)}, u32[]{:S(2)}) collective-permute-start(bf16[8,1024]{1,0:T(8,128)(2,1)S(1)} %slice.156), channel_id=1, source_target_pairs={{0,4},{1,5},{2,6},{3,7},{8,12},{9,13},{10,14},{11,15},{16,20},{17,... | collective-permute-start | bytes 49160 | tf_op jit(solution)/shard_map/ppermute | solution.py:819
  21.8 3.5 fusion.2
  28.7 38.1 %all-gather.4.cloned.1.call-done = bf16[1024,1024]{0,1:T(8,128)(2,1)} async-done(((bf16[128,1024]{0,1:T(8,128)(2,1)}), bf16[1024,1024]{0,1:T(8,128)(2,1)}) %all-gather.4.cloned.1.call-update) | async-done | bytes 2097168 | tf_op jit(solution)/shard_map/all_gather | solution.py:777
  66.8 6.8 %fusion.96.proj = f32[1024,1024]{1,0:T(8,128)} fusion(bf16[1024,1024]{1,0:T(8,128)(2,1)} %fusion.2, bf16[1024,1024]{0,1:T(8,128)(2,1)} %all-gather.4.cloned.1.call-done), kind=kOutput, calls=%fused_computation.265 | convolution fusion | flops 2147483648 | bytes 8388608 | tf_op jit(solution)/shard_map/dot_general | solution.py:34
  74.0 11.1 %shard_map.339 = (bf16[1024,128]{1,0:T(8,128)(2,1)S(1)}, bf16[1024,128]{1,0:T(8,128)(2,1)S(1)}, bf16[1024,640]{1,0:T(8,128)(2,1)S(1)}, f32[1024,640]{1,0:T(8,128...) custom-call(s32[5]{0:T(128)S(1)} %pad_add_fusion.meta, ...), custom_call_target="tpu_custom_call" | custom-call | tf_op jit(solution)/shard_map/pallas_call | solution.py:605
  91.6 3.8 shard_map.340.y_in
  102.3 6.1 %shard_map.341 = (bf16[1024,128]{1,0:T(8,128)(2,1)S(1)}, f32[1024,128]{1,0:T(8,128)S(1)}) custom-call(s32[5]{0:T(128)S(1)} %pad_add_fusion.meta, bf16[1024,128]{1,0:T(8,128)(2,1)S(1)} %copy-done.11, bf16[2048,128]{1,0:T(8,128)(2,1)S(1)} %bitcast.237), custom_call_target="tpu_custom_call" | custom-call | tf_op jit(solution)/shard_map/pallas_call | solution.py:605
  109.2 7.2 %all-gather.6.cloned.1.call-done = bf16[1024,896]{0,1:T(8,128)(2,1)} async-done(((bf16[128,896]{0,1:T(8,128)(2,1)}), bf16[1024,896]{0,1:T(8,128)(2,1)}) %all-gather.6.cloned.1.call-update) | async-done | bytes 1835024 | tf_op jit(solution)/shard_map/all_gather | solution.py:777
  116.4 4.3 %fusion.85.gate = f32[1024,384]{1,0:T(8,128)} fusion(bf16[1024,1024]{1,0:T(8,128)(2,1)} %fusion.2, bf16[1024,896]{0,1:T(8,128)(2,1)} %all-gather.6.cloned.1.call-done), kind=kOutput, calls=%fused_computation.259 | convolution fusion | flops 805306368 | bytes 4456448 | tf_op jit(solution)/shard_map/dot_general | solution.py:34
  120.7 5.2 %shard_map.342 = (bf16[1024,512]{1,0:T(8,128)(2,1)S(1)}, f32[1024,384]{1,0:T(8,128)S(1)}, f32[1536,128]{1,0:T(8,128)S(1)}) custom-call(s32[5]{0:T(128)S(1)} %pad_add_fusion.meta, f32[1024,384]{1,0:T(8,128)} %copy-done.3, f32[1024,640]{1,0:T(8,128)} %get-tuple-element.62.act, f32[1024,128]{1,0:T(8,128)S(1)} %get-tuple-element.64.cum, ...), custom_call_target="tpu_custom_call" | custom-call | tf_op jit(solution)/shard_map/pallas_call | solution.py:605
  139.4 13.8 %collective-permute-done.4 = bf16[1,256,1024]{2,1,0:T(8,128)(2,1)} collective-permute-done((bf16[1,256,1024]{2,1,0:T(8,128)(2,1)}, bf16[1,256,1024]{2,1,0:T(8,128)(2,1)}, u32[]{:S(2)}, u32[]{:S(2)}) %collective-permute-start.4) | collective-permute-done | bytes 524320 | tf_op jit(solution)/shard_map/ppermute | solution.py:638
  158.3 12.9 %collective-permute-done.5 = bf16[256,1024]{1,0:T(8,128)(2,1)} collective-permute-done((bf16[256,1024]{1,0:T(8,128)(2,1)}, bf16[256,1024]{1,0:T(8,128)(2,1)}, u32[]{:S(2)}, u32[]{:S(2)}) %collective-permute-start.5) | collective-permute-done | bytes 524320 | tf_op jit(solution)/shard_map/ppermute | solution.py:638
  182.2 11.2 %shard_map.343 = (bf16[1024,512]{1,0:T(8,128)(2,1)S(1)}, bf16[1024,1024]{1,0:T(8,128)(2,1)S(1)}, bf16[1024,1024]{1,0:T(8,128)(2,1)S(1)}, bf16[1024,1024]{1,0:T(8,128)(2,1)}) custom-call(bf16[1024,1024]{1,0:T(8,128)(2,1)} %bitcast.246, bf16[1024,1024]{1,0:T(8,128)(2,1)} %cotangent.1, bf16[1024,1536]{1,0:T(8,128)(2,1)} %all-gather.8.cloned.1.call-done.weights), custom_call_target="tpu_custom_call" | custom-call | tf_op jit(solution)/shard_map/pallas_call | solution.py:605
  202.6 10.4 %collective-permute-done.8 = bf16[1,256,1024]{2,1,0:T(8,128)(2,1)} collective-permute-done((bf16[1,256,1024]{2,1,0:T(8,128)(2,1)}, bf16[1,256,1024]{2,1,0:T(8,128)(2,1)}, u32[]{:S(2)}, u32[]{:S(2)}) %collective-permute-start.8) | collective-permute-done | bytes 524320 | tf_op jit(solution)/shard_map/ppermute | solution.py:638
  219.3 11.6 %collective-permute-done.9 = bf16[256,1024]{1,0:T(8,128)(2,1)S(1)} collective-permute-done((bf16[256,1024]{1,0:T(8,128)(2,1)S(1)}, bf16[256,1024]{1,0:T(8,128)(2,1)S(1)}, u32[]{:S(2)}, u32[]{:S(2)}) %collective-permute-start.9) | collective-permute-done | bytes 524320 | tf_op jit(solution)/shard_map/ppermute | solution.py:638
  243.4 6.7 %shard_map.344 = (f32[1024,384]{1,0:T(8,128)S(1)}, bf16[1024,384]{1,0:T(8,128)(2,1)S(1)}, f32[8,384]{1,0:T(8,128)S(1)}, f32[384,128]{1,0:T(8,128)S(1)}) custom-call(s32[5]{0:T(128)S(1)} %pad_add_fusion.meta, f32[1024,384]{1,0:T(8,128)S(1)} %slice.211.grad, f32[1024,384]{1,0:T(8,128)} %copy-done.4, f32[1024,640]{1,0:T(8,128)} %get-tuple-element.62.act, ...), custom_call_target="tpu_custom_call" | custom-call | tf_op jit(solution)/shard_map/pallas_call | solution.py:605
  253.4 9.1 %shard_map.345 = (bf16[1024,128]{1,0:T(8,128)(2,1)S(1)}, f32[2048,128]{1,0:T(8,128)S(1)}) custom-call(s32[5]{0:T(128)S(1)} %pad_add_fusion.meta, bf16[1024,128]{1,0:T(8,128)(2,1)S(1)} %copy-done.12, bf16[2048,128]{1,0:T(8,128)(2,1)S(1)} %bitcast.238, f32[1024,128]{1,0:T(8,128)S(1)} %slice.212.grad, bf16[1024,128]{1,0:T(8,128)(2,1)S(1)} %get-tuple-element.67.att, ...), custom_call_target="tpu_custom_call" | custom-call | tf_op jit(solution)/shard_map/pallas_call | solution.py:605
  271.7 5.2 %collective-permute-done.17 = bf16[1,1024,128]{2,1,0:T(8,128)(2,1)} collective-permute-done((bf16[1,1024,128]{2,1,0:T(8,128)(2,1)}, bf16[1,1024,128]{2,1,0:T(8,128)(2,1)}, u32[]{:S(2)}, u32[]{:S(2)}) %collective-permute-start.17) | collective-permute-done | bytes 262176 | tf_op jit(solution)/shard_map/ppermute | solution.py:638
  284.0 16.8 %shard_map.346 = (bf16[1024,640]{1,0:T(8,128)(2,1)S(1)}, bf16[1024,128]{1,0:T(8,128)(2,1)S(1)}, f32[8,640]{1,0:T(8,128)S(1)}, f32[8,640]{1,0:T(8,128)S(1)}, f32[8,640]{1,0:T(8,128)S(1)}, /*index=5*/f32[8,128]{1,0:T(8,128)S(1)}) custom-call(s32[5]{0:T(128)S(1)} %pad_add_fusion.meta, f32[1024,640]{1,0:T(8,128)} %get-tuple-element.62.act, ...), custom_call_target="tpu_custom_call" | custom-call | tf_op jit(solution)/shard_map/pallas_call | solution.py:605
  329.9 3.3 convolution_convert_fusion.1
  333.3 17.7 %collective-permute-done.27 = bf16[2,2,128,384]{3,2,1,0:T(8,128)(2,1)S(1)} collective-permute-done((bf16[2,2,128,384]{3,2,1,0:T(8,128)(2,1)S(1)}, bf16[2,2,128,384]{3,2,1,0:T(8,128)(2,1)S(1)}, u32[]{:S(2)}, u32[]{:S(2)}) %collective-permute-start.27) | collective-permute-done | bytes 393248 | tf_op jit(solution)/shard_map/ppermute | solution.py:638
  364.1 5.6 %collective-permute-done.23 = f32[8,1408]{1,0:T(8,128)S(1)} collective-permute-done((f32[8,1408]{1,0:T(8,128)S(1)}, f32[8,1408]{1,0:T(8,128)S(1)}, u32[]{:S(2)}, u32[]{:S(2)}) %collective-permute-start.23) | collective-permute-done | bytes 45088 | tf_op jit(solution)/shard_map/ppermute | solution.py:638
  377.2 7.9 %collective-permute-done.25 = f32[8,1408]{1,0:T(8,128)S(1)} collective-permute-done((f32[8,1408]{1,0:T(8,128)S(1)}, f32[8,1408]{1,0:T(8,128)S(1)}, u32[]{:S(2)}, u32[]{:S(2)}) %collective-permute-start.25) | collective-permute-done | bytes 45088 | tf_op jit(solution)/shard_map/ppermute | solution.py:638
  393.0 4.0 collective-permute-done.32
  (418 shorter events, 179.3 us)
Async XLA Ops:
  7.2 59.5 %all-gather.4.cloned.1.call-start = ((), (), s32[]{:S(2)}) async-start(), calls=%async_computation.2 | async-start | bytes 2359296 | tf_op jit(solution)/shard_map/all_gather | solution.py:777
  12.9 103.6 %all-gather.6.cloned.1.call-start = ((), (), s32[]{:S(2)}) async-start(), calls=%async_computation.3 | async-start | bytes 2064384 | tf_op jit(solution)/shard_map/all_gather | solution.py:777
  14.6 167.6 %all-gather.8.cloned.1.call-start = ((), (), s32[]{:S(2)}) async-start(), calls=%async_computation.4 | async-start | bytes 3538944 | tf_op jit(solution)/shard_map/all_gather | solution.py:777
  14.6 13.9 %collective-permute-start = (bf16[8,1024]{1,0:T(8,128)(2,1)S(1)}, bf16[8,1024]{1,0:T(8,128)(2,1)S(1)}, u32[]{:S(2)}, u32[]{:S(2)}) collective-permute-start(bf16[8,1024]{1,0:T(8,128)(2,1)S(1)} %slice.156), channel_id=1, source_target_pairs={{0,4},{1,5},{2,6},{3,7},{8,12},{9,13},{10,14},{11,15},{16,20},{17,... | collective-permute-start | bytes 49160 | tf_op jit(solution)/shard_map/ppermute | solution.py:819
  20.5 378.8 %reduce-scatter.5.cloned.1.call-start = ((), (), s32[]{:S(2)}) async-start(), calls=%async_computation.6 | async-start | bytes 3538944 | tf_op jit(solution)/shard_map/reduce_scatter | solution.py:967
  138.9 14.3 %collective-permute-start.4 = (bf16[1,256,1024]{2,1,0:T(8,128)(2,1)}, bf16[1,256,1024]{2,1,0:T(8,128)(2,1)}, u32[]{:S(2)}, u32[]{:S(2)}) collective-permute-start(bf16[1,256,1024]{2,1,0:T(8,128)(2,1)} %dynamic-slice_bitcast_fusion.4), channel_id=1, source_target_pairs={{0,2},{1,3},{2,0},{3,1},{4,6},{5,7},{6,4},{7,5},{8,10},{9,11},{10,... | collective-permute-start | bytes 1572872 | tf_op jit(solution)/shard_map/ppermute | solution.py:638
  157.8 13.4 %collective-permute-start.5 = (bf16[256,1024]{1,0:T(8,128)(2,1)}, bf16[256,1024]{1,0:T(8,128)(2,1)}, u32[]{:S(2)}, u32[]{:S(2)}) collective-permute-start(bf16[256,1024]{1,0:T(8,128)(2,1)} %multiply_convert_fusion), channel_id=1, source_target_pairs={{0,2},{1,3},{2,0},{3,1},{4,6},{5,7},{6,4},{7,5},{8,10},{9,11},{10,... | collective-permute-start | bytes 1572872 | tf_op jit(solution)/shard_map/ppermute | solution.py:638
  198.7 14.3 %collective-permute-start.8 = (bf16[1,256,1024]{2,1,0:T(8,128)(2,1)}, bf16[1,256,1024]{2,1,0:T(8,128)(2,1)}, u32[]{:S(2)}, u32[]{:S(2)}) collective-permute-start(bf16[1,256,1024]{2,1,0:T(8,128)(2,1)} %constant_dynamic-slice_fusion.6), channel_id=1, source_target_pairs={{0,2},{1,3},{2,0},{3,1},{4,6},{5,7},{6,4},{7,5},{8,10},{9,11},{10,... | collective-permute-start | bytes 1572872 | tf_op jit(solution)/shard_map/ppermute | solution.py:638
  217.7 13.2 %collective-permute-start.9 = (bf16[256,1024]{1,0:T(8,128)(2,1)S(1)}, bf16[256,1024]{1,0:T(8,128)(2,1)S(1)}, u32[]{:S(2)}, u32[]{:S(2)}) collective-permute-start(bf16[256,1024]{1,0:T(8,128)(2,1)S(1)} %convert_element_type.457), channel_id=1, source_target_pairs={{0,2},{1,3},{2,0},{3,1},{4,6},{5,7},{6,4},{7,5},{8,10},{9,11},{10,... | collective-permute-start | bytes 1572872 | tf_op jit(solution)/shard_map/ppermute | solution.py:638
  219.3 15.8 %collective-permute-start.12 = (bf16[2,256,1024]{2,1,0:T(8,128)(2,1)}, bf16[2,256,1024]{2,1,0:T(8,128)(2,1)}, u32[]{:S(2)}, u32[]{:S(2)}) collective-permute-start(bf16[2,256,1024]{2,1,0:T(8,128)(2,1)} %dynamic-slice_bitcast_fusion), channel_id=1, source_target_pairs={{0,1},{1,0},{2,3},{3,2},{4,5},{5,4},{6,7},{7,6},{8,9},{9,8},{10,11... | collective-permute-start | bytes 3145736 | tf_op jit(solution)/shard_map/ppermute | solution.py:638
  235.1 172.9 %reduce-scatter.3.cloned.1.call-start = ((), (), s32[]{:S(2)}) async-start(), calls=%async_computation.5 | async-start | bytes 2359296 | tf_op jit(solution)/shard_map/reduce_scatter | solution.py:1030
  242.9 35.1 %collective-permute-start.13 = (bf16[1,256,1024]{2,1,0:T(8,128)(2,1)}, bf16[1,256,1024]{2,1,0:T(8,128)(2,1)}, u32[]{:S(2)}, u32[]{:S(2)}) collective-permute-start(bf16[1,256,1024]{2,1,0:T(8,128)(2,1)} %constant_dynamic-slice_fusion.5), channel_id=1, source_target_pairs={{0,2},{1,3},{2,0},{3,1},{4,6},{5,7},{6,4},{7,5},{8,10},{9,11},{10,... | collective-permute-start | bytes 1572872 | tf_op jit(solution)/shard_map/ppermute | solution.py:638
  252.0 18.5 %collective-permute-start.11 = (bf16[400,128]{1,0:T(8,128)(2,1)}, bf16[400,128]{1,0:T(8,128)(2,1)}, u32[]{:S(2)}, u32[]{:S(2)}) collective-permute-start(bf16[400,128]{1,0:T(8,128)(2,1)} %pad_maximum_fusion.23), channel_id=1, source_target_pairs={{0,4},{4,0},{1,5},{5,1},{2,6},{6,2},{3,7},{7,3},{8,12},{12,8},{9,1... | collective-permute-start | bytes 307208 | tf_op jit(solution)/shard_map/ppermute | solution.py:638
  263.3 13.6 %collective-permute-start.17 = (bf16[1,1024,128]{2,1,0:T(8,128)(2,1)}, bf16[1,1024,128]{2,1,0:T(8,128)(2,1)}, u32[]{:S(2)}, u32[]{:S(2)}) collective-permute-start(bf16[1,1024,128]{2,1,0:T(8,128)(2,1)} %dynamic-slice_bitcast_fusion.7), channel_id=1, source_target_pairs={{0,4},{4,0},{1,5},{5,1},{2,6},{6,2},{3,7},{7,3},{8,12},{12,8},{9,1... | collective-permute-start | bytes 786440 | tf_op jit(solution)/shard_map/ppermute | solution.py:638
  302.6 17.0 %collective-permute-start.14 = (bf16[256,1024]{1,0:T(8,128)(2,1)}, bf16[256,1024]{1,0:T(8,128)(2,1)S(1)}, u32[]{:S(2)}, u32[]{:S(2)}) collective-permute-start(bf16[256,1024]{1,0:T(8,128)(2,1)} %fusion.38), channel_id=1, source_target_pairs={{0,2},{1,3},{2,0},{3,1},{4,6},{5,7},{6,4},{7,5},{8,10},{9,11},{10,... | collective-permute-start | bytes 1572872 | tf_op jit(solution)/shard_map/ppermute | solution.py:638
  321.8 30.7 %collective-permute-start.15 = (bf16[2,256,1024]{2,1,0:T(8,128)(2,1)}, bf16[2,256,1024]{2,1,0:T(8,128)(2,1)S(1)}, u32[]{:S(2)}, u32[]{:S(2)}) collective-permute-start(bf16[2,256,1024]{2,1,0:T(8,128)(2,1)} %pad_maximum_fusion.15), channel_id=1, source_target_pairs={{0,1},{1,0},{2,3},{3,2},{4,5},{5,4},{6,7},{7,6},{8,9},{9,8},{10,11... | collective-permute-start | bytes 3145736 | tf_op jit(solution)/shard_map/ppermute | solution.py:638
  325.0 29.3 %collective-permute-start.19 = (bf16[1,256,1024]{2,1,0:T(8,128)(2,1)}, bf16[1,256,1024]{2,1,0:T(8,128)(2,1)}, u32[]{:S(2)}, u32[]{:S(2)}) collective-permute-start(bf16[1,256,1024]{2,1,0:T(8,128)(2,1)} %dynamic-slice_bitcast_fusion.3), channel_id=1, source_target_pairs={{0,2},{1,3},{2,0},{3,1},{4,6},{5,7},{6,4},{7,5},{8,10},{9,11},{10,... | collective-permute-start | bytes 1572872 | tf_op jit(solution)/shard_map/ppermute | solution.py:638
  329.8 21.2 %collective-permute-start.27 = (bf16[2,2,128,384]{3,2,1,0:T(8,128)(2,1)S(1)}, bf16[2,2,128,384]{3,2,1,0:T(8,128)(2,1)S(1)}, u32[]{:S(2)}, u32[]{:S(2)}) collective-permute-start(bf16[2,2,128,384]{3,2,1,0:T(8,128)(2,1)S(1)} %dynamic-slice_bitcast_fusion.5), channel_id=1, source_target_pairs={{0,8},{8,0},{16,24},{24,16},{1,9},{9,1},{17,25},{25,17},{2,10},{10... | collective-permute-start | bytes 1179656 | tf_op jit(solution)/shard_map/ppermute | solution.py:638
  333.3 24.3 %collective-permute-start.30 = (bf16[4,1,128,512]{3,2,0,1:T(8,128)(2,1)S(1)}, bf16[4,1,128,512]{3,2,0,1:T(8,128)(2,1)S(1)}, u32[]{:S(2)}, u32[]{:S(2)}) collective-permute-start(bf16[4,1,128,512]{3,2,0,1:T(8,128)(2,1)S(1)} %dynamic-slice_bitcast_fusion.2), channel_id=1, source_target_pairs={{0,4},{4,0},{1,5},{5,1},{2,6},{6,2},{3,7},{7,3},{8,12},{12,8},{9,1... | collective-permute-start | bytes 1572872 | tf_op jit(solution)/shard_map/ppermute | solution.py:638
  352.2 11.7 %collective-permute-start.28 = (bf16[1,2,128,384]{3,2,1,0:T(8,128)(2,1)S(1)}, bf16[1,2,128,384]{3,2,1,0:T(8,128)(2,1)S(1)}, u32[]{:S(2)}, u32[]{:S(2)}) collective-permute-start(bf16[1,2,128,384]{3,2,1,0:T(8,128)(2,1)S(1)} %constant_dynamic-slice_fusion.2), channel_id=1, source_target_pairs={{0,16},{8,24},{16,0},{24,8},{1,17},{9,25},{17,1},{25,9},{2,18},{10... | collective-permute-start | bytes 589832 | tf_op jit(solution)/shard_map/ppermute | solution.py:638
  357.8 27.4 %collective-permute-start.31 = (bf16[2,1,128,512]{3,2,1,0:T(8,128)(2,1)S(1)}, bf16[2,1,128,512]{3,2,1,0:T(8,128)(2,1)S(1)}, u32[]{:S(2)}, u32[]{:S(2)}) collective-permute-start(bf16[2,1,128,512]{3,2,1,0:T(8,128)(2,1)S(1)} %dynamic-slice_bitcast_fusion.6), channel_id=1, source_target_pairs={{0,8},{8,0},{16,24},{24,16},{1,9},{9,1},{17,25},{25,17},{2,10},{10... | collective-permute-start | bytes 786440 | tf_op jit(solution)/shard_map/ppermute | solution.py:638
  364.0 12.4 %collective-permute-start.29 = (bf16[1,1,128,384]{3,2,1,0:T(8,128)(2,1)S(1)}, bf16[1,1,128,384]{3,2,1,0:T(8,128)(2,1)S(1)}, u32[]{:S(2)}, u32[]{:S(2)}) collective-permute-start(bf16[1,1,128,384]{3,2,1,0:T(8,128)(2,1)S(1)} %constant_dynamic-slice_fusion.1), channel_id=1, source_target_pairs={{0,4},{4,0},{1,5},{5,1},{2,6},{6,2},{3,7},{7,3},{8,12},{12,8},{9,1... | collective-permute-start | bytes 294920 | tf_op jit(solution)/shard_map/ppermute | solution.py:638
  370.2 17.8 %collective-permute-start.20 = (bf16[256,1024]{1,0:T(8,128)(2,1)S(1)}, bf16[256,1024]{1,0:T(8,128)(2,1)S(1)}, u32[]{:S(2)}, u32[]{:S(2)}) collective-permute-start(bf16[256,1024]{1,0:T(8,128)(2,1)S(1)} %fusion.28), channel_id=1, source_target_pairs={{0,2},{1,3},{2,0},{3,1},{4,6},{5,7},{6,4},{7,5},{8,10},{9,11},{10,... | collective-permute-start | bytes 1572872 | tf_op jit(solution)/shard_map/ppermute | solution.py:638
  385.3 11.7 %collective-permute-start.32 = (bf16[1,1,128,512]{3,2,1,0:T(8,128)(2,1)S(1)}, bf16[1,1,128,512]{3,2,1,0:T(8,128)(2,1)S(1)}, u32[]{:S(2)}, u32[]{:S(2)}) collective-permute-start(bf16[1,1,128,512]{3,2,1,0:T(8,128)(2,1)S(1)} %constant_dynamic-slice_fusion), channel_id=1, source_target_pairs={{0,16},{8,24},{16,0},{24,8},{1,17},{9,25},{17,1},{25,9},{2,18},{10... | collective-permute-start | bytes 393224 | tf_op jit(solution)/shard_map/ppermute | solution.py:638
  (87 other events, 424.4 us)
Sparse Core Ops, SparseCore 0:
  13.0 53.7 all-gather.3
  69.4 46.9 all-gather.5
  119.2 58.3 all-gather.7
  235.2 75.6 reduce-scatter.4
  317.5 78.9 reduce-scatter.2
